TPU v7x, 32 devices: a whole 2x2x4 slice. The times are simulated.
32 devices in a mesh: seq: 4 (over x, core), vocab: 8 (over z, y).
Axes of the slice: x: 2, y: 2, z: 4, core: 2. Of those that a mesh axis runs over, the one named last changes fastest.
Arguments:
- hidden: bfloat16 [512, 8192], P('seq'), may hold values from -6 to 6
- steer: float32 [8192], replicated, may hold values from -4 to 4
- tangent: float32 [8192], replicated, may hold values from -6 to 6
- gain: float32 [8192], replicated, may hold values from 0.5 to 1.5
- head: bfloat16 [8192, 19456], P('seq', 'vocab'), may hold values from -0.198873782 to 0.198873782
- target: bfloat16 [512, 19456], P('seq', 'vocab'), may hold values from 0.099609375 to 10
Outputs:
- gradient: float32 [512, 8192], P('vocab', 'seq')
- curvature: float32 [512, 8192], P('vocab', 'seq')
All inputs are finite; a program needn't handle non-finite values.
Results may differ from a plain program's by a relative error of at most 0.0082.
Values may be sent and summed in bfloat16 or wider, within the bound.
No kernel may reach another device: no remote copies, remote signals or barrier semaphores. Data moves between devices by JAX's collectives and lax.ppermute only.
A program may use at most 128 MiB of HBM per device.

v0:
```python
import jax
import jax.numpy as jnp
from jax import lax
from jax.sharding import PartitionSpec as P

EPSILON = 1e-06


def norm_back(inputs, radius, denominator, gain_part, upstream_grad, upstream_ggn, feature_count):
    scaled_grad = gain_part * upstream_grad
    scaled_ggn = gain_part * upstream_ggn
    dot_grad, dot_ggn = lax.psum(
        (jnp.sum(inputs * scaled_grad, axis=1), jnp.sum(inputs * scaled_ggn, axis=1)), "seq"
    )
    result_grad = (
        scaled_grad - inputs * (dot_grad / feature_count / denominator)[:, None]
    ) / radius[:, None]
    result_ggn = (scaled_ggn - inputs * (dot_ggn / feature_count / denominator)[:, None]) / radius[
        :, None
    ]
    return (result_grad, result_ggn)


def body(hidden, steer, tangent, gain, head, target):
    seq_index = lax.axis_index("seq")
    feature_count = hidden.shape[1]
    slice_width = head.shape[0]
    vocab_width = head.shape[1]
    relaid = lax.all_to_all(hidden, "seq", split_axis=1, concat_axis=0, tiled=True)
    offset = seq_index * slice_width
    steer_part = lax.dynamic_slice_in_dim(steer, offset, slice_width)
    tangent_part = lax.dynamic_slice_in_dim(tangent, offset, slice_width)
    gain_part = lax.dynamic_slice_in_dim(gain, offset, slice_width)
    inputs = relaid.astype(jnp.float32) + steer_part
    sum_squares, sum_tangent = lax.psum(
        (jnp.sum(inputs * inputs, axis=1), jnp.sum(inputs * tangent_part, axis=1)), "seq"
    )
    denominator = sum_squares / feature_count + EPSILON
    radius = jnp.sqrt(denominator)
    tangent_dot = sum_tangent / feature_count
    normed = (gain_part * inputs / radius[:, None]).astype(jnp.bfloat16)
    tangent_normed = (
        gain_part * (tangent_part - inputs * (tangent_dot / denominator)[:, None]) / radius[:, None]
    ).astype(jnp.bfloat16)
    both_logits = lax.psum_scatter(
        jnp.concatenate(
            [
                jnp.dot(normed, head, preferred_element_type=jnp.float32),
                jnp.dot(tangent_normed, head, preferred_element_type=jnp.float32),
            ],
            axis=1,
        ),
        "seq",
        scatter_dimension=0,
        tiled=True,
    )
    logits = both_logits[:, :vocab_width]
    dlogits = both_logits[:, vocab_width:]
    weights = target.astype(jnp.float32)
    local_peak = jnp.max(logits, axis=1)
    row_peak = lax.pmax(local_peak, "vocab")
    exponent = jnp.exp(logits - row_peak[:, None])
    row_total, shift_total, weight_total = lax.psum(
        (jnp.sum(exponent, axis=1), jnp.sum(exponent * dlogits, axis=1), jnp.sum(weights, axis=1)),
        "vocab",
    )
    softmax_probs = exponent / row_total[:, None]
    mean_shift = shift_total / row_total
    target_probs = weights / weight_total[:, None]
    cot_grad = (softmax_probs - target_probs).astype(jnp.bfloat16)
    cot_ggn = (softmax_probs * (dlogits - mean_shift[:, None])).astype(jnp.bfloat16)
    cotangent = jnp.concatenate([cot_grad, cot_ggn], axis=1)
    gathered = lax.all_gather(cotangent, "seq", axis=0, tiled=True)
    dims = (((1,), (1,)), ((), ()))
    share_rows = gathered.shape[0] // lax.axis_size("vocab")
    start_row = lax.axis_index("vocab") * share_rows
    first_part = lax.dot_general(
        gathered[:, :vocab_width], head, dims, preferred_element_type=jnp.float32
    )
    second_part = lax.dot_general(
        gathered[:, vocab_width:], head, dims, preferred_element_type=jnp.float32
    )
    mine = lax.psum_scatter(
        jnp.concatenate([first_part, second_part], axis=1), "vocab", scatter_dimension=0, tiled=True
    )
    inputs_rows = lax.dynamic_slice_in_dim(inputs, start_row, share_rows, 0)
    radius_rows = lax.dynamic_slice_in_dim(radius, start_row, share_rows, 0)
    denominator_rows = lax.dynamic_slice_in_dim(denominator, start_row, share_rows, 0)
    grad_part, ggn_part = norm_back(
        inputs_rows,
        radius_rows,
        denominator_rows,
        gain_part,
        mine[:, :slice_width],
        mine[:, slice_width:],
        feature_count,
    )
    return (grad_part, ggn_part)


def solution(mesh):
    return jax.shard_map(
        body,
        mesh=mesh,
        in_specs=(P("seq", None), P(), P(), P(), P("seq", "vocab"), P("seq", "vocab")),
        out_specs=(P("vocab", "seq"), P("vocab", "seq")),
        check_vma=False,
    )
```

profile of v0, /device:TPU:0, one launch (start us, length us, event | category | flops | bytes accessed | tf_op | source)
XLA Modules:
  0.0 425.1 jit_solution(18398159004895099202)
XLA Ops:
  7.2 3.2 copy.12
  10.4 4.2 all-to-all-start
  15.3 0.7 dynamic_slice.19
  16.7 23.6 %all-to-all-done = bf16[128,4,2048]{2,0,1:T(8,128)(2,1)S(1)} async-done(((bf16[128,4,2048]{2,0,1:T(8,128)(2,1)}), bf16[128,4,2048]{2,0,1:T(8,128)(2,1)S(1)}, u32[]{:S(2)}, u32[]{:S(2)}) %all-to-all-start) | async-done | bytes 2097184 | tf_op jit(solution)/shard_map/all_to_all | solution.py:29
  40.3 0.9 multiply_reduce_fusion.1
  41.2 5.8 %all-reduce.2 = (f32[512]{0:T(512)S(1)}, f32[512]{0:T(512)S(1)}) all-reduce(f32[512]{0:T(512)S(1)} %bitcast.21, f32[512]{0:T(512)S(1)} %bitcast.20), channel_id=1, replica_groups=mesh['seq'=4,'vocab'=8] {'seq'}, use_global_device_ids=true, to_apply=%region_3.0 | all-reduce | flops 1024 | bytes 8192 | tf_op jit(solution)/shard_map/psum | solution.py:35
  47.6 10.5 %fusion.5 = f32[512,2432]{1,0:T(8,128)S(1)} fusion(bf16[2048,2432]{1,0:T(8,128)(2,1)} %param.10, f32[512,2048]{1,0:T(8,128)S(1)} %bitcast_add_fusion, f32[512]{0:T(512)S(1)} %get-tuple-element.22, f32[2048]{0:T(1024)S(1)} %dynamic_slice.18), kind=kOutput, calls=%fused_computation.12 | convolution fusion | flops 5103419392 | bytes 19146752 | tf_op jit(solution)/shard_map/dot_general | solution.py:48
  58.2 7.6 %fusion.4 = f32[512,2432]{1,0:T(8,128)} fusion(bf16[2048,2432]{1,0:T(8,128)(2,1)S(1)} %bitcast.23, f32[512,2048]{1,0:T(8,128)S(1)} %bitcast_add_fusion, f32[512]{0:T(512)S(1)} %get-tuple-element.23, f32[2048]{0:T(1024)S(1)} %dynamic_slice.20, f32[512]{0:T(512)S(1)} %get-tuple-element.22, f32[2048]{0:T(1024)S(1)} %dynamic_slice.18), kind=kOutput, calls=%fused_computation.11 | convolution fusion | flops 5105516544 | bytes 19156992 | tf_op jit(solution)/shard_map/dot_general | solution.py:49
  65.8 6.9 %pad_maximum_fusion = f32[512,4864]{1,0:T(8,128)} fusion(f32[512,2432]{1,0:T(8,128)} %fusion.4, f32[512,2432]{1,0:T(8,128)S(1)} %fusion.5), kind=kLoop, calls=%fused_computation | loop fusion | flops 2490368 | bytes 19922944 | tf_op jit(solution)/shard_map/concatenate | solution.py:46
  72.7 1.0 copy-done.2
  73.9 82.5 %reduce-scatter.3.cloned.1.call-done = f32[128,4864]{1,0:T(8,128)} async-done(((f32[512,4864]{1,0:T(8,128)}), f32[128,4864]{1,0:T(8,128)}) %reduce-scatter.3.cloned.1.call-update) | async-done | bytes 2490384 | tf_op jit(solution)/shard_map/reduce_scatter | solution.py:45
  156.4 1.6 slice_reduce_fusion
  158.0 21.4 %pmax.7 = f32[128]{0:T(128)S(1)} all-reduce(f32[128]{0:T(128)S(1)} %slice_reduce_fusion), channel_id=1, replica_groups=mesh['seq'=4,'vocab'=8] {'vocab'}, use_global_device_ids=true, to_apply=%region_6.0 | all-reduce | flops 128 | bytes 1024 | tf_op jit(solution)/shard_map/pmax | solution.py:61
  179.4 2.1 fusion.15
  181.4 17.1 %all-reduce = (f32[128]{0:T(128)S(1)}, f32[128]{0:T(128)S(1)}, f32[128]{0:T(128)S(1)}) all-reduce(f32[128]{0:T(128)S(1)} %get-tuple-element.5, f32[128]{0:T(128)S(1)} %get-tuple-element.4, f32[128]{0:T(128)S(1)} %convert_reduce_fusion), channel_id=1, replica_groups=mesh['seq'=4,'vocab'=8] {'vocab'}, use_global_device_ids=true, to_apply=%region_12.0 | all-reduce | flops 384 | bytes 3072 | tf_op jit(solution)/shard_map/psum | solution.py:63
  199.1 1.1 pad_maximum_fusion.2
  200.5 36.6 %all-gather.2.cloned.1.call-done = bf16[512,4864]{1,0:T(8,128)(2,1)} async-done(((bf16[128,4864]{1,0:T(8,128)(2,1)}), bf16[512,4864]{1,0:T(8,128)(2,1)}) %all-gather.2.cloned.1.call-update) | async-done | bytes 4980752 | tf_op jit(solution)/shard_map/all_gather | solution.py:73
  237.2 9.2 %fusion = f32[512,2048]{1,0:T(8,128)S(1)} fusion(bf16[2048,2432]{1,0:T(8,128)(2,1)} %param.10, bf16[512,4864]{1,0:T(8,128)(2,1)} %all-gather.2.cloned.1.call-done), kind=kOutput, calls=%fused_computation.7 | convolution fusion | flops 5100273664 | bytes 16646144 | tf_op jit(solution)/shard_map/dot_general | solution.py:80
  246.3 8.2 %fusion.2 = f32[512,2048]{1,0:T(8,128)S(1)} fusion(bf16[2048,2432]{1,0:T(8,128)(2,1)} %param.10, bf16[512,4864]{1,0:T(8,128)(2,1)S(1)} %copy-done.3), kind=kOutput, calls=%fused_computation.9 | convolution fusion | flops 5100273664 | bytes 16646144 | tf_op jit(solution)/shard_map/dot_general | solution.py:77
  254.6 3.8 pad_maximum_fusion.1
  258.5 149.1 %reduce-scatter.5.cloned.1.call-done = f32[64,4096]{1,0:T(8,128)} async-done(((f32[512,4096]{1,0:T(8,128)}), f32[64,4096]{1,0:T(8,128)}) %reduce-scatter.5.cloned.1.call-update) | async-done | bytes 1048592 | tf_op jit(solution)/shard_map/reduce_scatter | solution.py:83
  407.6 1.6 multiply_reduce_fusion.3
  409.1 6.8 %all-reduce.1 = (f32[64]{0:T(128)S(1)}, f32[64]{0:T(128)S(1)}) all-reduce(f32[64]{0:T(128)S(1)} %get-tuple-element.3, f32[64]{0:T(128)S(1)} %get-tuple-element.2), channel_id=1, replica_groups=mesh['seq'=4,'vocab'=8] {'seq'}, use_global_device_ids=true, to_apply=%region_15.0 | all-reduce | flops 128 | bytes 1024 | tf_op jit(solution)/shard_map/psum | solution.py:12
  416.0 2.5 subtract_divide_fusion
  (29 shorter events, 3.2 us)
Async XLA Ops:
  10.4 29.9 %all-to-all-start = ((bf16[128,4,2048]{2,0,1:T(8,128)(2,1)}), bf16[128,4,2048]{2,0,1:T(8,128)(2,1)S(1)}, u32[]{:S(2)}, u32[]{:S(2)}) async-start(bf16[128,4,2048]{2,0,1:T(8,128)(2,1)} %bitcast.18), calls=%async_computation | async-start | bytes 4194304 | tf_op jit(solution)/shard_map/all_to_all | solution.py:29
  14.6 141.9 %reduce-scatter.3.cloned.1.call-start = ((), (), s32[]{:S(2)}) async-start(), calls=%async_computation.3 | async-start | bytes 12451840 | tf_op jit(solution)/shard_map/reduce_scatter | solution.py:45
  47.0 11.2 %slice-start = ((s8[9961472]{0:T(1024)(128)(4,1)}), s8[4194304]{0:T(1024)(128)(4,1)S(1)}, s32[]{:S(2)}) async-start(s8[9961472]{0:T(1024)(128)(4,1)} %bitcast.22), calls=%async_computation.6 | async-start | bytes 8388608
  47.5 10.6 %copy-start.1 = (f32[512,2048]{1,0:T(8,128)}, f32[512,2048]{1,0:T(8,128)S(1)}, u32[]{:S(2)}) copy-start(f32[512,2048]{1,0:T(8,128)S(1)} %bitcast_add_fusion) | copy-start | bytes 12582916
  47.5 10.6 %slice-start.1 = ((s8[9961472]{0:T(1024)(128)(4,1)}), s8[4194304]{0:T(1024)(128)(4,1)S(1)}, s32[]{:S(2)}) async-start(s8[9961472]{0:T(1024)(128)(4,1)} %bitcast.22), calls=%async_computation.7 | async-start | bytes 8388608
  47.6 10.6 %slice-start.2 = ((s8[9961472]{0:T(1024)(128)(4,1)}), s8[1572864]{0:T(1024)(128)(4,1)S(1)}, s32[]{:S(2)}) async-start(s8[9961472]{0:T(1024)(128)(4,1)} %bitcast.22), calls=%async_computation.8 | async-start | bytes 3145728
  72.7 1.1 copy-start.2
  72.7 164.5 %all-gather.2.cloned.1.call-start = ((), (), s32[]{:S(2)}) async-start(), calls=%async_computation.4 | async-start | bytes 6225920 | tf_op jit(solution)/shard_map/all_gather | solution.py:73
  156.4 42.2 %copy-start = (f32[128,4864]{1,0:T(8,128)S(1)}, f32[128,4864]{1,0:T(8,128)}, u32[]{:S(2)}) copy-start(f32[128,4864]{1,0:T(8,128)} %reduce-scatter.3.cloned.1.call-done) | copy-start | bytes 7471108
  200.3 207.3 %reduce-scatter.5.cloned.1.call-start = ((), (), s32[]{:S(2)}) async-start(), calls=%async_computation.5 | async-start | bytes 9437184 | tf_op jit(solution)/shard_map/reduce_scatter | solution.py:83
  237.2 9.2 %copy-start.3 = (bf16[512,4864]{1,0:T(8,128)(2,1)S(1)}, bf16[512,4864]{1,0:T(8,128)(2,1)}, u32[]{:S(2)}) copy-start(bf16[512,4864]{1,0:T(8,128)(2,1)} %all-gather.2.cloned.1.call-done) | copy-start | bytes 14942212
Sparse Core Ops, SparseCore 0:
  72.8 83.5 reduce-scatter.2
  200.4 36.7 all-gather.1
  258.5 149.0 reduce-scatter.4
where the time goes:
time: 426 us; the launch traced here: 425 us
  waiting for transfers between devices  292 us (69%)
  blocking collectives  51.1 us (12%)
  matrix products  35.5 us (8%)
  other arithmetic  21.8 us (5%)
  between operations  13.9 us (3%)
  local copies, waits for them, and re-layouts  6.39 us (2%)
  starting transfers between devices  4.47 us (1%)
    reduce_scatter x1, waiting for transfers between devices, body(): lax.psum_scatter(jnp.concatenate([first_part, second_part], axis=1), 'voc...  149 us
    reduce_scatter x1, waiting for transfers between devices, body(): lax.psum_scatter(jnp.concatenate([jnp.dot(normed, head, preferred_element...  82.5 us
    all_gather x1, waiting for transfers between devices, body(): gathered = lax.all_gather(cotangent, 'seq', axis=0, tiled=True)  36.6 us
    all_to_all x1, waiting for transfers between devices, body(): lax.all_to_all(hidden, 'seq', split_axis=1, concat_axis=0, tiled=True)  23.6 us
    pmax x1, blocking collectives, body(): row_peak = lax.pmax(local_peak, 'vocab')  21.4 us
    psum x1, blocking collectives, body(): lax.psum((jnp.sum(exponent, axis=1), jnp.sum(exponent * dlogits, axis=1),...  17.1 us
    dot_general x1, matrix products, body(): jnp.dot(normed, head, preferred_element_type=jnp.float32)  10.5 us
    dot_general x1, matrix products, body(): lax.dot_general(gathered[:, vocab_width:], head, dims, preferred_element_...  9.17 us
  transfers between devices with their start and end apart: 4, of which 4 were waited for; matrix products, arithmetic and copies ran while one was open for 1% of the time, Pallas kernels for 0%

commit v1 on v0

v1 whole, which is shorter than its diff:
```python
import jax
import jax.numpy as jnp
from jax import lax
from jax.sharding import PartitionSpec as P

EPSILON = 1e-06
ROWS_BY_ROWS = (((1,), (1,)), ((), ()))


def swap(value, axis, bit, size):
    return lax.ppermute(value, axis, [(i, i ^ bit) for i in range(size)])


def shift(value, axis, pairs):
    return lax.ppermute(value, axis, pairs)


def chain_scatter(parts, place, length, pair):
    def right(step):
        return [
            (z * pair + y, (z + 1) * pair + y)
            for z in range(length - 1)
            for y in range(pair)
            if z < step
        ]

    def left(step):
        return [
            ((length - 1 - z) * pair + y, (length - 2 - z) * pair + y)
            for z in range(length - 1)
            for y in range(pair)
            if z < step
        ]

    going_up = going_down = None
    for step in range(1, length):
        up = lax.dynamic_index_in_dim(parts, length - step + place, 0, False)
        down = lax.dynamic_index_in_dim(parts, step - length + place, 0, False)
        if step > 1:
            up = up + going_up.astype(jnp.float32)
            down = down + going_down.astype(jnp.float32)
        going_up = shift(up.astype(jnp.bfloat16), "vocab", right(step))
        going_down = shift(down.astype(jnp.bfloat16), "vocab", left(step))
    own = lax.dynamic_index_in_dim(parts, place, 0, False)
    return own + going_up.astype(jnp.float32) + going_down.astype(jnp.float32)


def vocab_scatter(partial, seq_index, vocab_index, vocab_size):
    blocks, rows, features = partial.shape
    pair = 2
    length = vocab_size // pair
    share = blocks * rows // vocab_size
    cut = partial.reshape(blocks, length // blocks, pair, share, features)
    mine_y = vocab_index % pair
    theirs = lax.dynamic_index_in_dim(cut, 1 - mine_y, 2, False).astype(jnp.bfloat16)
    got = swap(theirs, "vocab", 1, vocab_size)
    kept = lax.dynamic_index_in_dim(cut, mine_y, 2, False) + got.astype(jnp.float32)
    order = jnp.bitwise_xor(jnp.arange(blocks), seq_index)
    kept = jnp.take(kept, order, axis=0).reshape(length, share, features)
    return chain_scatter(kept, vocab_index // pair, length, pair)


def body(hidden, steer, tangent, gain, head, target):
    seq_size = lax.axis_size("seq")
    vocab_size = lax.axis_size("vocab")
    seq_index = lax.axis_index("seq")
    vocab_index = lax.axis_index("vocab")
    tokens, feature_count = hidden.shape
    width = head.shape[0]
    float32, bfloat16 = jnp.float32, jnp.bfloat16

    blocks = []
    for bit in range(seq_size):
        cut = lax.dynamic_slice_in_dim(hidden, (seq_index ^ bit) * width, width, 1)
        blocks.append(cut if bit == 0 else swap(cut, "seq", bit, seq_size))

    inputs = hidden.astype(float32) + steer
    sums = jnp.stack([jnp.sum(inputs * inputs, axis=1), jnp.sum(inputs * tangent, axis=1)])
    all_sums = jnp.stack(
        [sums if bit == 0 else swap(sums, "seq", bit, seq_size) for bit in range(seq_size)], axis=1
    )
    denominator = all_sums[0] / feature_count + EPSILON
    radius = jnp.sqrt(denominator)
    slope = all_sums[1] / feature_count / denominator

    offset = seq_index * width
    steer_part = lax.dynamic_slice_in_dim(steer, offset, width)
    tangent_part = lax.dynamic_slice_in_dim(tangent, offset, width)
    gain_part = lax.dynamic_slice_in_dim(gain, offset, width)

    line = gain_part * tangent_part
    high = line.astype(bfloat16)
    low = (line - high.astype(float32)).astype(bfloat16)
    two = jnp.concatenate(
        [high[None], low[None], jnp.zeros((14, width), bfloat16)], axis=0
    )
    row = jnp.sum(jnp.dot(two, head, preferred_element_type=float32), axis=0)
    tangent_row = row
    for bit in range(1, seq_size):
        tangent_row = tangent_row + swap(row, "seq", bit, seq_size)

    def partial_logits(bit):
        values = blocks[bit].astype(float32) + steer_part
        normed = (gain_part * values / radius[bit][:, None]).astype(bfloat16)
        return jnp.dot(normed, head, preferred_element_type=float32)

    logits = [None] * 4
    sums_of = {}
    got_of = {}
    for base in (0, 2):
        kept = partial_logits(base)
        given = partial_logits(base + 1)
        whole = kept + swap(given, "seq", 1, seq_size)
        sums_of[base] = whole
        got_of[base ^ 2] = swap(whole.astype(jnp.float16), "seq", 2, seq_size)
    for base in (2, 0):
        full = sums_of[base] + got_of[base].astype(float32)
        logits[base] = full
        logits[base + 1] = swap(full, "seq", 1, seq_size)
    logits = jnp.stack(logits)

    target_1 = swap(target, "seq", 1, seq_size)
    target_2 = swap(target, "seq", 2, seq_size)
    target_3 = swap(target_2, "seq", 1, seq_size)
    weights = jnp.stack([target, target_1, target_2, target_3])

    peak = jnp.max(logits, axis=2)
    below = logits - peak[..., None]
    exponent = jnp.exp(below)
    dlogits = tangent_row / radius[..., None] - logits * slope[..., None]
    total = jnp.sum(exponent, axis=2)
    shift_mean = jnp.sum(exponent * dlogits, axis=2) / total
    tilted = exponent * (dlogits - shift_mean[..., None])
    total_below = jnp.sum(exponent * below, axis=2)
    tilted_below = jnp.sum(tilted * below, axis=2)
    wide = weights.astype(float32)
    weight_sum = jnp.sum(wide, axis=2)
    weight_logits = jnp.sum(wide * logits, axis=2)

    stats = lax.all_gather(
        jnp.stack([peak, total, shift_mean, total_below, tilted_below, weight_sum, weight_logits]),
        "vocab",
    )
    peaks, totals, means, belows, tilts, weight_sums, weight_lines = (
        stats[:, i] for i in range(7)
    )
    row_peak = jnp.max(peaks, axis=0)
    factor = jnp.exp(peaks - row_peak)
    row_total = jnp.sum(factor * totals, axis=0)
    mean_shift = jnp.sum(factor * totals * means, axis=0) / row_total
    first = belows + peaks * totals
    weight_total = jnp.sum(weight_sums, axis=0)
    dot_grad = (
        jnp.sum(factor * first, axis=0) / row_total - jnp.sum(weight_lines, axis=0) / weight_total
    )
    dot_ggn = jnp.sum(factor * (tilts + (means - mean_shift) * first), axis=0) / row_total
    scale = jnp.exp(peak - row_peak) / row_total
    lean = scale * (shift_mean - mean_shift)

    rows = seq_size * tokens

    def back(cotangent):
        flat = cotangent.astype(bfloat16).reshape(rows, -1)
        out = lax.dot_general(flat, head, ROWS_BY_ROWS, preferred_element_type=float32)
        return out.reshape(seq_size, tokens, width)

    back_plain = back(exponent)
    back_tilted = back(tilted)
    back_weights = back(weights)
    ggn = scale[..., None] * back_tilted + lean[..., None] * back_plain
    ggn_mine = vocab_scatter(ggn, seq_index, vocab_index, vocab_size)
    grad = scale[..., None] * back_plain - back_weights / weight_total[..., None]
    grad_mine = vocab_scatter(grad, seq_index, vocab_index, vocab_size)

    share = rows // vocab_size
    owner = vocab_index * share // tokens
    inner = vocab_index * share - owner * tokens
    block = jnp.bitwise_xor(owner, seq_index)

    def mine(values):
        return lax.dynamic_slice(values, (block, inner), (1, share))[0]

    my_hidden = lax.dynamic_slice(jnp.stack(blocks), (block, inner, 0), (1, share, width))[0]
    my_inputs = my_hidden.astype(float32) + steer_part
    my_radius, my_denominator = mine(radius), mine(denominator)

    def norm_back(upstream, dotted):
        along = dotted * my_radius / feature_count / my_denominator
        return (gain_part * upstream - my_inputs * along[:, None]) / my_radius[:, None]

    return norm_back(grad_mine, mine(dot_grad)), norm_back(ggn_mine, mine(dot_ggn))


def solution(mesh):
    return jax.shard_map(
        body,
        mesh=mesh,
        in_specs=(P("seq", None), P(), P(), P(), P("seq", "vocab"), P("seq", "vocab")),
        out_specs=(P("vocab", "seq"), P("vocab", "seq")),
        check_vma=False,
    )
```

time: 426 us -> 264 us (0.62)
  waiting for transfers between devices: 292 us -> 106 us
  starting transfers between devices: 4.47 us -> 42.1 us
  blocking collectives: 51.1 us -> 30.6 us
  between operations: 13.9 us -> 1.34 us
  matrix products: 35.5 us -> 44.7 us
  local copies, waits for them, and re-layouts: 6.39 us -> 12.2 us
  other arithmetic: 21.8 us -> 26.6 us
    reduce_scatter x2 -> x0, waiting for transfers between devices: 232 us -> none  [the longest x1 149 us: body(): lax.psum_scatter(jnp.concatenate([first_part, second_part], axis=1), 'voc...]
    ppermute x0 -> x32, waiting for transfers between devices: none -> 106 us  [the longest x20 89.1 us: swap(): return lax.ppermute(value, axis, [(i, i ^ bit) for i in range(size)])]
    ppermute x0 -> x32, starting transfers between devices: none -> 42.1 us  [the longest x12 25.4 us: shift(): return lax.ppermute(value, axis, pairs)]
    all_gather x1 -> x0, waiting for transfers between devices: 36.6 us -> none  [body(): gathered = lax.all_gather(cotangent, 'seq', axis=0, tiled=True)]
    all_gather x0 -> x1, blocking collectives: none -> 30.6 us  [body(): lax.all_gather(jnp.stack([peak, total, shift_mean, total_below, tilted_be...]
    psum x3 -> x0, blocking collectives: 29.7 us -> none  [the longest x1 17.1 us: body(): lax.psum((jnp.sum(exponent, axis=1), jnp.sum(exponent * dlogits, axis=1),...]
    all_to_all x1 -> x0, waiting for transfers between devices: 23.6 us -> none  [body(): lax.all_to_all(hidden, 'seq', split_axis=1, concat_axis=0, tiled=True)]
    pmax x1 -> x0, blocking collectives: 21.4 us -> none  [body(): row_peak = lax.pmax(local_peak, 'vocab')]
  transfers between devices with their start and end apart: 4 -> 32, of which waited for: 4 -> 16; matrix products, arithmetic and copies ran while one was open for 1% -> 10% of each run, Pallas kernels for 0% -> 0%
where the time goes in v1:
time: 264 us
  waiting for transfers between devices  106 us (40%)
  matrix products  44.7 us (17%)
  starting transfers between devices  42.1 us (16%)
  blocking collectives  30.6 us (12%)
  other arithmetic  26.6 us (10%)
  local copies, waits for them, and re-layouts  12.2 us (5%)
    ppermute x20, waiting for transfers between devices, swap(): return lax.ppermute(value, axis, [(i, i ^ bit) for i in range(size)])  89.1 us
    dot_general x3, matrix products, back(): lax.dot_general(flat, head, ROWS_BY_ROWS, preferred_element_type=float32)  31.7 us
    all_gather x1, blocking collectives, body(): lax.all_gather(jnp.stack([peak, total, shift_mean, total_below, tilted_be...  30.6 us
    ppermute x12, starting transfers between devices, shift(): return lax.ppermute(value, axis, pairs)  25.4 us
    ppermute x12, waiting for transfers between devices, shift(): return lax.ppermute(value, axis, pairs)  16.8 us
    ppermute x20, starting transfers between devices, swap(): return lax.ppermute(value, axis, [(i, i ^ bit) for i in range(size)])  16.7 us
    dot_general x4, matrix products, partial_logits(): return jnp.dot(normed, head, preferred_element_type=float32)  11.5 us
    reduce_sum x1, other arithmetic, body(): tilted_below = jnp.sum(tilted * below, axis=2)  5.29 us
  transfers between devices with their start and end apart: 32, of which 16 were waited for; matrix products, arithmetic and copies ran while one was open for 10% of the time, Pallas kernels for 0%

profile of v1, /device:TPU:0, one launch (start us, length us, event | category | flops | bytes accessed | tf_op | source)
XLA Modules:
  0.0 263.5 jit_solution(16689628550065070085)
XLA Ops:
  3.2 3.0 %collective-permute-start.1 = (f32[2,128]{1,0:T(2,128)S(1)}, f32[2,128]{1,0:T(2,128)S(1)}, u32[]{:S(2)}, u32[]{:S(2)}) collective-permute-start(f32[2,128]{1,0:T(2,128)S(1)} %get-tuple-element.51), channel_id=1, source_target_pairs={{0,16},{8,24},{16,0},{24,8},{1,17},{9,25},{17,1},{25,9},{2,18},{10... | collective-permute-start | bytes 3080 | tf_op jit(solution)/shard_map/ppermute | solution.py:11
  12.1 10.8 %collective-permute-done.6 = bf16[128,2048]{1,0:T(8,128)(2,1)S(1)} collective-permute-done((bf16[128,2048]{1,0:T(8,128)(2,1)S(1)}, bf16[128,2048]{1,0:T(8,128)(2,1)S(1)}, u32[]{:S(2)}, u32[]{:S(2)}) %collective-permute-start.6) | collective-permute-done | bytes 524320 | tf_op jit(solution)/shard_map/ppermute | solution.py:11
  22.9 5.7 %fusion.25 = f32[128,2432]{1,0:T(8,128)S(1)} fusion(bf16[2048,2432]{1,0:T(8,128)(2,1)} %param.12, bf16[128,2048]{1,0:T(8,128)(2,1)S(1)} %collective-permute-done.6, f32[128]{0:T(128)S(1)} %get-tuple-element.47, f32[2048]{0:T(1024)S(1)} %dynamic_slice.94, f32[2048]{0:T(1024)S(1)} %get-tuple-element.43), kind=kOutput, calls=%fused_computation.57 | convolution fusion | flops 1276379136 | bytes 11747840 | tf_op jit(solution)/shard_map/dot_general | solution.py:105
  34.3 9.2 %collective-permute-done.5 = bf16[128,2048]{1,0:T(8,128)(2,1)S(1)} collective-permute-done((bf16[128,2048]{1,0:T(8,128)(2,1)S(1)}, bf16[128,2048]{1,0:T(8,128)(2,1)S(1)}, u32[]{:S(2)}, u32[]{:S(2)}) %collective-permute-start.5) | collective-permute-done | bytes 524320 | tf_op jit(solution)/shard_map/ppermute | solution.py:11
  47.0 13.8 %collective-permute-done.8 = f16[128,2432]{1,0:T(8,128)(2,1)S(1)} collective-permute-done((f16[128,2432]{1,0:T(8,128)(2,1)S(1)}, f16[128,2432]{1,0:T(8,128)(2,1)S(1)}, u32[]{:S(2)}, u32[]{:S(2)}) %collective-permute-start.8) | collective-permute-done | bytes 622624 | tf_op jit(solution)/shard_map/ppermute | solution.py:11
  65.6 14.9 %collective-permute-done.10 = f16[128,2432]{1,0:T(8,128)(2,1)S(1)} collective-permute-done((f16[128,2432]{1,0:T(8,128)(2,1)S(1)}, f16[128,2432]{1,0:T(8,128)(2,1)S(1)}, u32[]{:S(2)}, u32[]{:S(2)}) %collective-permute-start.10) | collective-permute-done | bytes 622624 | tf_op jit(solution)/shard_map/ppermute | solution.py:11
  81.3 10.3 %collective-permute-done.16 = bf16[128,2432]{1,0:T(8,128)(2,1)} collective-permute-done((bf16[128,2432]{1,0:T(8,128)(2,1)}, bf16[128,2432]{1,0:T(8,128)(2,1)}, u32[]{:S(2)}, u32[]{:S(2)}) %collective-permute-start.16) | collective-permute-done | bytes 622624 | tf_op jit(solution)/shard_map/ppermute | solution.py:11
  101.2 3.5 %fusion.6 = (f32[4,128]{1,0:T(4,128)S(1)}, f32[4,128]{1,0:T(4,128)S(1)}, f32[4,128]{1,0:T(4,128)S(1)}) fusion(bf16[1,128,2432]{2,1,0:T(8,128)(2,1)} %bitcast.24, bf16[1,128,2432]{2,1,0:T(8,128)(2,1)} %bitcast.23, bf16[1,128,2432]{2,1,0:T(8,128)(2,1)S(1)} %bitcast.253, bf16[1,128,2432]{2,1,0:T(8,128)(2,1)} %bitcast.21, f32[1,128,2432]{2,1,0:T(8,128)} %bitcast.13, ...), kind=kLoop, calls=%fused_computation.16 | loop fusion | flops 13695488 | bytes 7477248 | tf_op jit(solution)/shard_map/reduce_sum | solution.py:138
  104.7 4.5 %fusion.7 = (f32[4,128]{1,0:T(4,128)S(1)}, f32[4,128]{1,0:T(4,128)S(1)}) fusion(f32[4,128]{1,0:T(4,128)S(1)} %bitcast.261, f32[4,128]{1,0:T(4,128)S(1)} %bitcast.258, f32[2432]{0:T(1024)S(1)} %add_add_fusion, f32[4,128]{1,0:T(4,128)S(1)} %get-tuple-element.8, f32[1,128,2432]{2,1,0:T(8,128)} %bitcast.13, f32[1,128,2432]{2,1,0:T(8,128)S(1)} %bitcast.236, ...), kind=kLoop, calls=%fused_computation.17 | loop fusion | flops 12450816 | bytes 5000704 | tf_op jit(solution)/shard_map/reduce_sum | solution.py:132
  109.2 5.3 %multiply_reduce_fusion = (f32[4,128]{1,0:T(4,128)S(1)}, f32[4,128]{1,0:T(4,128)S(1)}) fusion(f32[4,128]{1,0:T(4,128)S(1)} %div.198, f32[4,128]{1,0:T(4,128)S(1)} %bitcast.262, f32[4,128]{1,0:T(4,128)S(1)} %bitcast.259, f32[2432]{0:T(1024)S(1)} %add_add_fusion, f32[4,128]{1,0:T(4,128)S(1)} %get-tuple-element.8, f32[1,128,2432]{2,1,0:T(8,128)} %bitcast.13, ...), kind=kLoop, calls=%fused_computation.20 | loop fusion | flops 16186368 | bytes 5002752 | tf_op jit(solution)/shard_map/reduce_sum | solution.py:135
  114.5 30.6 %all-gather = f32[56,4,128]{2,1,0:T(4,128)S(1)} all-gather(f32[7,4,128]{2,1,0:T(4,128)S(1)} %constant_dynamic-update-slice_fusion), channel_id=2, replica_groups=mesh['seq'=4,'vocab'=8] {'vocab'}, dimensions={0}, use_global_device_ids=true | all-gather | bytes 129024 | tf_op jit(solution)/shard_map/all_gather | solution.py:140
  145.2 12.2 %fusion.4 = f32[4,128,2048]{2,1,0:T(8,128)} fusion(bf16[2048,2432]{1,0:T(8,128)(2,1)} %param.12, f32[4,128]{1,0:T(4,128)S(1)} %get-tuple-element.8, f32[1,128,2432]{2,1,0:T(8,128)} %bitcast.13, f32[1,128,2432]{2,1,0:T(8,128)S(1)} %bitcast.238, f32[1,128,2432]{2,1,0:T(8,128)} %bitcast.11, f32[1,128,2432]{2,1,0:T(8,128)} %bitcast.243), kind=kOutput, calls=%fused_computation.6 | convolution fusion | flops 5106499584 | bytes 19138560 | tf_op jit(solution)/shard_map/dot_general | solution.py:164
  157.5 9.4 %divide_subtract_fusion.1 = f32[4,128,2048]{2,1,0:T(8,128)} fusion(f32[4,128,2048]{2,1,0:T(8,128)} %fusion.4, bf16[2048,2432]{1,0:T(8,128)(2,1)S(1)} %bitcast.234, f32[4,128]{1,0:T(4,128)S(1)} %get-tuple-element.17, f32[4,128]{1,0:T(4,128)S(1)} %get-tuple-element.24, bf16[1,128,2432]{2,1,0:T(8,128)(2,1)} %bitcast.24, bf16[1,128,2432]{2,1,0:T(8,128)(2,1)} %bitcast.23, ...), kind=kOutput, calls=%fused_computation.22 | convolution fusion | flops 5107154944 | bytes 20844544 | tf_op jit(solution)/shard_map/dot_general | solution.py:164
  166.9 2.7 %fusion.22 = bf16[4,1,64,2048]{3,2,0,1:T(8,128)(2,1)} fusion(f32[4,1,2,64,2048]{4,3,2,0,1:T(8,128)} %bitcast.247, s32[]{:T(128)S(6)} %select_n.105), kind=kLoop, calls=%fused_computation.50 | loop fusion | bytes 2097156 | tf_op jit(solution)/shard_map/convert_element_type | solution.py:55
  171.1 10.1 %multiply_add_fusion = f32[4,128,2048]{2,1,0:T(8,128)} fusion(f32[4,128,2048]{2,1,0:T(8,128)} %fusion.4, bf16[2048,2432]{1,0:T(8,128)(2,1)S(1)} %bitcast.234, f32[4,128]{1,0:T(4,128)S(1)} %div.198, f32[4,128]{1,0:T(4,128)S(1)} %bitcast.263, f32[4,128]{1,0:T(4,128)S(1)} %bitcast.260, f32[2432]{0:T(1024)S(1)} %add_add_fusion, ...), kind=kOutput, calls=%fused_computation.21 | convolution fusion | flops 5115871232 | bytes 23352832 | tf_op jit(solution)/shard_map/dot_general | solution.py:164
  183.7 12.3 %collective-permute-done.18 = bf16[4,1,64,2048]{3,2,0,1:T(8,128)(2,1)} collective-permute-done((bf16[4,1,64,2048]{3,2,0,1:T(8,128)(2,1)}, bf16[4,1,64,2048]{3,2,0,1:T(8,128)(2,1)}, u32[]{:S(2)}, u32[]{:S(2)}) %collective-permute-start.18) | collective-permute-done | bytes 1048608 | tf_op jit(solution)/shard_map/ppermute | solution.py:11
  200.2 11.1 %collective-permute-done.25 = bf16[4,1,64,2048]{3,2,0,1:T(8,128)(2,1)} collective-permute-done((bf16[4,1,64,2048]{3,2,0,1:T(8,128)(2,1)S(1)}, bf16[4,1,64,2048]{3,2,0,1:T(8,128)(2,1)}, u32[]{:S(2)}, u32[]{:S(2)}) %collective-permute-start.25) | collective-permute-done | bytes 1048608 | tf_op jit(solution)/shard_map/ppermute | solution.py:11
  215.4 2.7 %bitcast_select_fusion = (f32[4,1,64,2048]{3,2,1,0:T(8,128)S(1)}, f32[4,1,64,2048]{3,2,1,0:T(8,128)S(1)}) fusion(f32[4,64,2048]{2,1,0:T(8,128)} %gather_fusion.1, pred[4]{0:T(512)(128)(4,1)S(1)} %compare_and_fusion, f32[4,64,2048]{2,1,0:T(8,128)} %gather_fusion), kind=kLoop, calls=%fused_computation.39 | loop fusion | flops 1048576 | bytes 8388612 | tf_op jit(solution)/shard_map/jit(_take)/select_n | solution.py:59
  222.6 3.6 %collective-permute-done.26 = bf16[64,2048]{1,0:T(8,128)(2,1)S(1)} collective-permute-done((bf16[64,2048]{1,0:T(8,128)(2,1)S(1)}, bf16[64,2048]{1,0:T(8,128)(2,1)S(1)}, u32[]{:S(2)}, u32[]{:S(2)}) %collective-permute-start.26) | collective-permute-done | bytes 262176 | tf_op jit(solution)/shard_map/ppermute | solution.py:15
  226.2 4.4 %collective-permute-start.27 = (bf16[64,2048]{1,0:T(8,128)(2,1)S(1)}, bf16[64,2048]{1,0:T(8,128)(2,1)S(1)}, u32[]{:S(2)}, u32[]{:S(2)}) collective-permute-start(bf16[64,2048]{1,0:T(8,128)(2,1)S(1)} %fusion.34), channel_id=1, source_target_pairs={{0,2},{1,3},{2,4},{3,5},{8,10},{9,11},{10,12},{11,13},{16,18},{17,... | collective-permute-start | bytes 786440 | tf_op jit(solution)/shard_map/ppermute | solution.py:15
  231.8 4.4 %collective-permute-start.20 = (bf16[64,2048]{1,0:T(8,128)(2,1)S(1)}, bf16[64,2048]{1,0:T(8,128)(2,1)S(1)}, u32[]{:S(2)}, u32[]{:S(2)}) collective-permute-start(bf16[64,2048]{1,0:T(8,128)(2,1)S(1)} %fusion.40), channel_id=1, source_target_pairs={{0,2},{1,3},{2,4},{3,5},{8,10},{9,11},{10,12},{11,13},{16,18},{17,... | collective-permute-start | bytes 786440 | tf_op jit(solution)/shard_map/ppermute | solution.py:15
  237.5 4.4 %collective-permute-start.28 = (bf16[64,2048]{1,0:T(8,128)(2,1)S(1)}, bf16[64,2048]{1,0:T(8,128)(2,1)S(1)}, u32[]{:S(2)}, u32[]{:S(2)}) collective-permute-start(bf16[64,2048]{1,0:T(8,128)(2,1)S(1)} %get-tuple-element.33), channel_id=1, source_target_pairs={{0,2},{1,3},{2,4},{3,5},{4,6},{5,7},{8,10},{9,11},{10,12},{11,13},... | collective-permute-start | bytes 786440 | tf_op jit(solution)/shard_map/ppermute | solution.py:15
  242.7 4.2 %collective-permute-start.21 = (bf16[64,2048]{1,0:T(8,128)(2,1)S(1)}, bf16[64,2048]{1,0:T(8,128)(2,1)S(1)}, u32[]{:S(2)}, u32[]{:S(2)}) collective-permute-start(bf16[64,2048]{1,0:T(8,128)(2,1)S(1)} %get-tuple-element.37), channel_id=1, source_target_pairs={{0,2},{1,3},{2,4},{3,5},{4,6},{5,7},{8,10},{9,11},{10,12},{11,13},... | collective-permute-start | bytes 786440 | tf_op jit(solution)/shard_map/ppermute | solution.py:15
  250.4 8.7 %collective-permute-done.31 = bf16[64,2048]{1,0:T(8,128)(2,1)S(1)} collective-permute-done((bf16[64,2048]{1,0:T(8,128)(2,1)S(1)}, bf16[64,2048]{1,0:T(8,128)(2,1)S(1)}, u32[]{:S(2)}, u32[]{:S(2)}) %collective-permute-start.31) | collective-permute-done | bytes 262176 | tf_op jit(solution)/shard_map/ppermute | solution.py:15
  (137 shorter events, 60.3 us)
Async XLA Ops:
  3.2 8.9 %collective-permute-start.1 = (f32[2,128]{1,0:T(2,128)S(1)}, f32[2,128]{1,0:T(2,128)S(1)}, u32[]{:S(2)}, u32[]{:S(2)}) collective-permute-start(f32[2,128]{1,0:T(2,128)S(1)} %get-tuple-element.51), channel_id=1, source_target_pairs={{0,16},{8,24},{16,0},{24,8},{1,17},{9,25},{17,1},{25,9},{2,18},{10... | collective-permute-start | bytes 3080 | tf_op jit(solution)/shard_map/ppermute | solution.py:11
  9.1 13.8 %collective-permute-start.6 = (bf16[128,2048]{1,0:T(8,128)(2,1)S(1)}, bf16[128,2048]{1,0:T(8,128)(2,1)S(1)}, u32[]{:S(2)}, u32[]{:S(2)}) collective-permute-start(bf16[128,2048]{1,0:T(8,128)(2,1)S(1)} %get-tuple-element.31), channel_id=1, source_target_pairs={{0,24},{8,16},{16,8},{24,0},{1,25},{9,17},{17,9},{25,1},{2,26},{10... | collective-permute-start | bytes 1572872 | tf_op jit(solution)/shard_map/ppermute | solution.py:11
  28.6 14.9 %collective-permute-start.7 = (f32[128,2432]{1,0:T(8,128)S(1)}, f32[128,2432]{1,0:T(8,128)S(1)}, u32[]{:S(2)}, u32[]{:S(2)}) collective-permute-start(f32[128,2432]{1,0:T(8,128)S(1)} %fusion.25), channel_id=1, source_target_pairs={{0,8},{8,0},{16,24},{24,16},{1,9},{9,1},{17,25},{25,17},{2,10},{10... | collective-permute-start | bytes 3735560 | tf_op jit(solution)/shard_map/ppermute | solution.py:11
  29.2 14.4 %collective-permute-start.5 = (bf16[128,2048]{1,0:T(8,128)(2,1)S(1)}, bf16[128,2048]{1,0:T(8,128)(2,1)S(1)}, u32[]{:S(2)}, u32[]{:S(2)}) collective-permute-start(bf16[128,2048]{1,0:T(8,128)(2,1)S(1)} %get-tuple-element.32), channel_id=1, source_target_pairs={{0,16},{8,24},{16,0},{24,8},{1,17},{9,25},{17,1},{25,9},{2,18},{10... | collective-permute-start | bytes 1572872 | tf_op jit(solution)/shard_map/ppermute | solution.py:11
  34.0 13.0 %collective-permute-start.4 = (f32[128,2432]{1,0:T(8,128)S(1)}, f32[128,2432]{1,0:T(8,128)S(1)}, u32[]{:S(2)}, u32[]{:S(2)}) collective-permute-start(f32[128,2432]{1,0:T(8,128)S(1)} %fusion.24), channel_id=1, source_target_pairs={{0,8},{8,0},{16,24},{24,16},{1,9},{9,1},{17,25},{25,17},{2,10},{10... | collective-permute-start | bytes 3735560 | tf_op jit(solution)/shard_map/ppermute | solution.py:11
  45.2 15.6 %collective-permute-start.8 = (f16[128,2432]{1,0:T(8,128)(2,1)S(1)}, f16[128,2432]{1,0:T(8,128)(2,1)S(1)}, u32[]{:S(2)}, u32[]{:S(2)}) collective-permute-start(f16[128,2432]{1,0:T(8,128)(2,1)S(1)} %get-tuple-element.54), channel_id=1, source_target_pairs={{0,16},{8,24},{16,0},{24,8},{1,17},{9,25},{17,1},{25,9},{2,18},{10... | collective-permute-start | bytes 1867784 | tf_op jit(solution)/shard_map/ppermute | solution.py:11
  63.5 17.0 %collective-permute-start.10 = (f16[128,2432]{1,0:T(8,128)(2,1)S(1)}, f16[128,2432]{1,0:T(8,128)(2,1)S(1)}, u32[]{:S(2)}, u32[]{:S(2)}) collective-permute-start(f16[128,2432]{1,0:T(8,128)(2,1)S(1)} %get-tuple-element.42), channel_id=1, source_target_pairs={{0,16},{8,24},{16,0},{24,8},{1,17},{9,25},{17,1},{25,9},{2,18},{10... | collective-permute-start | bytes 1867784 | tf_op jit(solution)/shard_map/ppermute | solution.py:11
  64.9 26.7 %collective-permute-start.16 = (bf16[128,2432]{1,0:T(8,128)(2,1)}, bf16[128,2432]{1,0:T(8,128)(2,1)}, u32[]{:S(2)}, u32[]{:S(2)}) collective-permute-start(bf16[128,2432]{1,0:T(8,128)(2,1)} %param.13), channel_id=1, source_target_pairs={{0,16},{8,24},{16,0},{24,8},{1,17},{9,25},{17,1},{25,9},{2,18},{10... | collective-permute-start | bytes 1867784 | tf_op jit(solution)/shard_map/ppermute | solution.py:11
  65.6 35.6 %collective-permute-start.9 = (f32[128,2432]{1,0:T(8,128)S(1)}, f32[128,2432]{1,0:T(8,128)}, u32[]{:S(2)}, u32[]{:S(2)}) collective-permute-start(f32[128,2432]{1,0:T(8,128)S(1)} %get-tuple-element.41), channel_id=1, source_target_pairs={{0,8},{8,0},{16,24},{24,16},{1,9},{9,1},{17,25},{25,17},{2,10},{10... | collective-permute-start | bytes 3735560 | tf_op jit(solution)/shard_map/ppermute | solution.py:11
  80.6 20.6 %collective-permute-start.11 = (f32[128,2432]{1,0:T(8,128)S(1)}, f32[128,2432]{1,0:T(8,128)}, u32[]{:S(2)}, u32[]{:S(2)}) collective-permute-start(f32[128,2432]{1,0:T(8,128)S(1)} %convert_add_fusion.1), channel_id=1, source_target_pairs={{0,8},{8,0},{16,24},{24,16},{1,9},{9,1},{17,25},{25,17},{2,10},{10... | collective-permute-start | bytes 3735560 | tf_op jit(solution)/shard_map/ppermute | solution.py:11
  80.7 20.4 %collective-permute-start.15 = (bf16[128,2432]{1,0:T(8,128)(2,1)}, bf16[128,2432]{1,0:T(8,128)(2,1)S(1)}, u32[]{:S(2)}, u32[]{:S(2)}) collective-permute-start(bf16[128,2432]{1,0:T(8,128)(2,1)} %param.13), channel_id=1, source_target_pairs={{0,8},{8,0},{16,24},{24,16},{1,9},{9,1},{17,25},{25,17},{2,10},{10... | collective-permute-start | bytes 1867784 | tf_op jit(solution)/shard_map/ppermute | solution.py:11
  91.6 9.6 %collective-permute-start.17 = (bf16[128,2432]{1,0:T(8,128)(2,1)}, bf16[128,2432]{1,0:T(8,128)(2,1)}, u32[]{:S(2)}, u32[]{:S(2)}) collective-permute-start(bf16[128,2432]{1,0:T(8,128)(2,1)} %collective-permute-done.16), channel_id=1, source_target_pairs={{0,8},{8,0},{16,24},{24,16},{1,9},{9,1},{17,25},{25,17},{2,10},{10... | collective-permute-start | bytes 1867784 | tf_op jit(solution)/shard_map/ppermute | solution.py:11
  169.6 26.4 %collective-permute-start.18 = (bf16[4,1,64,2048]{3,2,0,1:T(8,128)(2,1)}, bf16[4,1,64,2048]{3,2,0,1:T(8,128)(2,1)}, u32[]{:S(2)}, u32[]{:S(2)}) collective-permute-start(bf16[4,1,64,2048]{3,2,0,1:T(8,128)(2,1)} %fusion.22), channel_id=1, source_target_pairs={{0,1},{1,0},{2,3},{3,2},{4,5},{5,4},{6,7},{7,6},{8,9},{9,8},{10,11... | collective-permute-start | bytes 3145736 | tf_op jit(solution)/shard_map/ppermute | solution.py:11
  182.9 28.3 %collective-permute-start.25 = (bf16[4,1,64,2048]{3,2,0,1:T(8,128)(2,1)S(1)}, bf16[4,1,64,2048]{3,2,0,1:T(8,128)(2,1)}, u32[]{:S(2)}, u32[]{:S(2)}) collective-permute-start(bf16[4,1,64,2048]{3,2,0,1:T(8,128)(2,1)S(1)} %fusion.23), channel_id=1, source_target_pairs={{0,1},{1,0},{2,3},{3,2},{4,5},{5,4},{6,7},{7,6},{8,9},{9,8},{10,11... | collective-permute-start | bytes 3145736 | tf_op jit(solution)/shard_map/ppermute | solution.py:11
  218.2 7.9 %collective-permute-start.26 = (bf16[64,2048]{1,0:T(8,128)(2,1)S(1)}, bf16[64,2048]{1,0:T(8,128)(2,1)S(1)}, u32[]{:S(2)}, u32[]{:S(2)}) collective-permute-start(bf16[64,2048]{1,0:T(8,128)(2,1)S(1)} %get-tuple-element.35), channel_id=1, source_target_pairs={{0,2},{1,3},{8,10},{9,11},{16,18},{17,19},{24,26},{25,27}} | collective-permute-start | bytes 786440 | tf_op jit(solution)/shard_map/ppermute | solution.py:15
  219.6 16.6 %collective-permute-start.29 = (bf16[64,2048]{1,0:T(8,128)(2,1)S(1)}, bf16[64,2048]{1,0:T(8,128)(2,1)S(1)}, u32[]{:S(2)}, u32[]{:S(2)}) collective-permute-start(bf16[64,2048]{1,0:T(8,128)(2,1)S(1)} %get-tuple-element.36), channel_id=1, source_target_pairs={{6,4},{7,5},{14,12},{15,13},{22,20},{23,21},{30,28},{31,29}} | collective-permute-start | bytes 786440 | tf_op jit(solution)/shard_map/ppermute | solution.py:15
  220.4 11.4 %collective-permute-start.19 = (bf16[64,2048]{1,0:T(8,128)(2,1)S(1)}, bf16[64,2048]{1,0:T(8,128)(2,1)S(1)}, u32[]{:S(2)}, u32[]{:S(2)}) collective-permute-start(bf16[64,2048]{1,0:T(8,128)(2,1)S(1)} %get-tuple-element.39), channel_id=1, source_target_pairs={{0,2},{1,3},{8,10},{9,11},{16,18},{17,19},{24,26},{25,27}} | collective-permute-start | bytes 786440 | tf_op jit(solution)/shard_map/ppermute | solution.py:15
  221.7 20.9 %collective-permute-start.22 = (bf16[64,2048]{1,0:T(8,128)(2,1)S(1)}, bf16[64,2048]{1,0:T(8,128)(2,1)S(1)}, u32[]{:S(2)}, u32[]{:S(2)}) collective-permute-start(bf16[64,2048]{1,0:T(8,128)(2,1)S(1)} %get-tuple-element.40), channel_id=1, source_target_pairs={{6,4},{7,5},{14,12},{15,13},{22,20},{23,21},{30,28},{31,29}} | collective-permute-start | bytes 786440 | tf_op jit(solution)/shard_map/ppermute | solution.py:15
  226.2 11.2 %collective-permute-start.27 = (bf16[64,2048]{1,0:T(8,128)(2,1)S(1)}, bf16[64,2048]{1,0:T(8,128)(2,1)S(1)}, u32[]{:S(2)}, u32[]{:S(2)}) collective-permute-start(bf16[64,2048]{1,0:T(8,128)(2,1)S(1)} %fusion.34), channel_id=1, source_target_pairs={{0,2},{1,3},{2,4},{3,5},{8,10},{9,11},{10,12},{11,13},{16,18},{17,... | collective-permute-start | bytes 786440 | tf_op jit(solution)/shard_map/ppermute | solution.py:15
  231.8 10.8 %collective-permute-start.20 = (bf16[64,2048]{1,0:T(8,128)(2,1)S(1)}, bf16[64,2048]{1,0:T(8,128)(2,1)S(1)}, u32[]{:S(2)}, u32[]{:S(2)}) collective-permute-start(bf16[64,2048]{1,0:T(8,128)(2,1)S(1)} %fusion.40), channel_id=1, source_target_pairs={{0,2},{1,3},{2,4},{3,5},{8,10},{9,11},{10,12},{11,13},{16,18},{17,... | collective-permute-start | bytes 786440 | tf_op jit(solution)/shard_map/ppermute | solution.py:15
  237.5 12.9 %collective-permute-start.28 = (bf16[64,2048]{1,0:T(8,128)(2,1)S(1)}, bf16[64,2048]{1,0:T(8,128)(2,1)S(1)}, u32[]{:S(2)}, u32[]{:S(2)}) collective-permute-start(bf16[64,2048]{1,0:T(8,128)(2,1)S(1)} %get-tuple-element.33), channel_id=1, source_target_pairs={{0,2},{1,3},{2,4},{3,5},{4,6},{5,7},{8,10},{9,11},{10,12},{11,13},... | collective-permute-start | bytes 786440 | tf_op jit(solution)/shard_map/ppermute | solution.py:15
  242.7 17.6 %collective-permute-start.21 = (bf16[64,2048]{1,0:T(8,128)(2,1)S(1)}, bf16[64,2048]{1,0:T(8,128)(2,1)S(1)}, u32[]{:S(2)}, u32[]{:S(2)}) collective-permute-start(bf16[64,2048]{1,0:T(8,128)(2,1)S(1)} %get-tuple-element.37), channel_id=1, source_target_pairs={{0,2},{1,3},{2,4},{3,5},{4,6},{5,7},{8,10},{9,11},{10,12},{11,13},... | collective-permute-start | bytes 786440 | tf_op jit(solution)/shard_map/ppermute | solution.py:15
  247.7 11.4 %collective-permute-start.31 = (bf16[64,2048]{1,0:T(8,128)(2,1)S(1)}, bf16[64,2048]{1,0:T(8,128)(2,1)S(1)}, u32[]{:S(2)}, u32[]{:S(2)}) collective-permute-start(bf16[64,2048]{1,0:T(8,128)(2,1)S(1)} %fusion.33), channel_id=1, source_target_pairs={{6,4},{7,5},{4,2},{5,3},{2,0},{3,1},{14,12},{15,13},{12,10},{13,11... | collective-permute-start | bytes 786440 | tf_op jit(solution)/shard_map/ppermute | solution.py:15
  249.1 13.4 %collective-permute-start.24 = (bf16[64,2048]{1,0:T(8,128)(2,1)S(1)}, bf16[64,2048]{1,0:T(8,128)(2,1)S(1)}, u32[]{:S(2)}, u32[]{:S(2)}) collective-permute-start(bf16[64,2048]{1,0:T(8,128)(2,1)S(1)} %fusion.39), channel_id=1, source_target_pairs={{6,4},{7,5},{4,2},{5,3},{2,0},{3,1},{14,12},{15,13},{12,10},{13,11... | collective-permute-start | bytes 786440 | tf_op jit(solution)/shard_map/ppermute | solution.py:15
  (24 other events, 373.4 us)

commit v2 on v0

v2 whole, which is shorter than its diff:
```python
import functools

import jax
import jax.numpy as jnp
from jax import lax
from jax.experimental import pallas as pl
from jax.experimental.pallas import tpu as pltpu
from jax.sharding import PartitionSpec as P

EPSILON = 1e-06
NT = (((1,), (1,)), ((), ()))
QUARTERS = 4
PAIR = 2
F32, BF16 = jnp.float32, jnp.bfloat16
VMEM_BYTES = 48 * 1024 * 1024


def params():
    return pltpu.CompilerParams(vmem_limit_bytes=VMEM_BYTES)


def whole_spec():
    return pl.BlockSpec(memory_space=pltpu.VMEM)


def smem_spec():
    return pl.BlockSpec(memory_space=pltpu.SMEM)


def swap(value, axis, bit, size):
    return lax.ppermute(value, axis, [(i, i ^ bit) for i in range(size)])


def lanes(columns, rows):
    lane = lax.broadcasted_iota(jnp.int32, (rows, 128), 1)
    tile = jnp.zeros((rows, 128), F32)
    for index, column in enumerate(columns):
        tile = jnp.where(lane == index, column, tile)
    return tile


def turn(rows8):
    return jnp.concatenate([rows8, jnp.zeros((120, 128), F32)], axis=0).T


def cut_kernel(width, seq_size, at, hidden, vectors, *outs):
    own, mate, near_2, near_3, far_2, far_3, sums, parts, two = outs
    seq_index, group = at[0], at[1]
    rows = hidden.shape[0]
    size = rows // QUARTERS

    def quarter(place):
        return pl.ds(pl.multiple_of((place ^ group) * size, size), size)

    def features(bit):
        return pl.ds(pl.multiple_of((seq_index ^ bit) * width, width), width)

    near_2[...] = hidden[quarter(0), features(2)]
    near_3[...] = hidden[quarter(0), features(3)]
    far_2[...] = hidden[quarter(3), features(2)]
    far_3[...] = hidden[quarter(3), features(3)]
    steer, tangent = vectors[0:1, :], vectors[1:2, :]
    columns = []
    for place in range(QUARTERS):
        spot = pl.ds(place * size, size)
        own[spot, :] = hidden[quarter(place), features(0)]
        mate[spot, :] = hidden[quarter(place), features(1)]
        inputs = hidden[quarter(place), :].astype(F32) + steer
        columns.append(
            lanes(
                [
                    jnp.sum(inputs * inputs, axis=1, keepdims=True),
                    jnp.sum(inputs * tangent, axis=1, keepdims=True),
                ],
                size,
            )
        )
    sums[...] = jnp.concatenate(columns, axis=0).T[:8]
    mine = vectors[:, features(0)]
    parts[...] = mine
    line = mine[1:2] * mine[2:3]
    high = line.astype(BF16).astype(F32)
    two[...] = jnp.concatenate(
        [high, line - high, jnp.zeros((14, width), F32)], axis=0
    ).astype(BF16)


def cut(at, hidden, vectors, width, seq_size):
    rows = hidden.shape[0]
    piece = jax.ShapeDtypeStruct((rows // QUARTERS, width), BF16)
    block = jax.ShapeDtypeStruct((rows, width), BF16)
    return pl.pallas_call(
        functools.partial(cut_kernel, width, seq_size),
        in_specs=[smem_spec(), whole_spec(), whole_spec()],
        out_specs=[whole_spec()] * 9,
        out_shape=[
            block,
            block,
            piece,
            piece,
            piece,
            piece,
            jax.ShapeDtypeStruct((8, rows), F32),
            jax.ShapeDtypeStruct((vectors.shape[0], width), F32),
            jax.ShapeDtypeStruct((16, width), BF16),
        ],
        compiler_params=params(),
    )(at, hidden, vectors)


def soften_kernel(feature_count, at, first, second, row, sums_a, sums_b, *outs):
    exponent_out, tilted_out, logits_out, stats, tile = outs
    tokens = first.shape[0]
    count = at.shape[0]
    size = 2 * tokens // count
    line = row[0:1, :]
    for block, (source, sums) in enumerate(((first, sums_a), (second, sums_b))):
        turned = turn(sums[...])
        denominator = turned[:, 0:1] / feature_count + EPSILON
        inverse = 1.0 / jnp.sqrt(denominator)
        slope = turned[:, 1:2] / feature_count / denominator
        for piece in range(count // 2):
            begin = piece * size
            logits = source[begin : begin + size, :]
            spot = pl.ds(pl.multiple_of(at[block * (count // 2) + piece], size), size)
            logits_out[spot, :] = logits
            peak = jnp.max(logits, axis=1, keepdims=True)
            below = logits - peak
            exponent = jnp.exp(below)
            dlogits = line * inverse[begin : begin + size] - logits * slope[begin : begin + size]
            total = jnp.sum(exponent, axis=1, keepdims=True)
            mean = jnp.sum(exponent * dlogits, axis=1, keepdims=True) / total
            tilted = exponent * (dlogits - mean)
            under = jnp.sum(exponent * below, axis=1, keepdims=True)
            tilted_under = jnp.sum(tilted * below, axis=1, keepdims=True)
            exponent_out[spot, :] = exponent.astype(BF16)
            tilted_out[spot, :] = tilted.astype(BF16)
            tile[spot, :] = lanes(
                [peak, total, mean, under + peak * total, tilted_under], size
            )
    for begin in range(0, 2 * tokens, 128):
        stats[:, begin : begin + 128] = tile[begin : begin + 128, :].T[:8]


def soften(at, first, second, row, sums_a, sums_b, feature_count):
    tokens, width = first.shape
    rows = 2 * tokens
    return pl.pallas_call(
        functools.partial(soften_kernel, feature_count),
        in_specs=[smem_spec()] + [whole_spec()] * 5,
        out_specs=[whole_spec()] * 4,
        out_shape=[
            jax.ShapeDtypeStruct((rows, width), BF16),
            jax.ShapeDtypeStruct((rows, width), BF16),
            jax.ShapeDtypeStruct((rows, width), F32),
            jax.ShapeDtypeStruct((8, rows), F32),
        ],
        scratch_shapes=[pltpu.VMEM((rows, 128), F32)],
        compiler_params=params(),
        cost_estimate=pl.CostEstimate(
            flops=30 * rows * width, bytes_accessed=12 * rows * width, transcendentals=rows * width
        ),
    )(at, first, second, row, sums_a, sums_b)


def weigh_kernel(at, *refs):
    blocks, (logits_own, logits_other), (ordered_own, ordered_other, stats, tile) = (
        refs[:4],
        refs[4:6],
        refs[6:],
    )
    tokens = blocks[0].shape[0]
    count = at.shape[0]
    size = 4 * tokens // count
    half = 2 * tokens
    for block in range(4):
        logits, ordered = (
            (logits_own, ordered_own) if block < 2 else (logits_other, ordered_other)
        )
        for piece in range(count // 4):
            begin = piece * size
            value = blocks[block][begin : begin + size, :]
            place = pl.multiple_of(at[block * (count // 4) + piece], size)
            spot = pl.ds(place, size)
            ordered[spot, :] = value
            wide = value.astype(F32)
            tile[pl.ds(place + half * (block // 2), size), :] = lanes(
                [
                    jnp.sum(wide, axis=1, keepdims=True),
                    jnp.sum(wide * logits[spot, :], axis=1, keepdims=True),
                ],
                size,
            )
    for begin in range(0, 2 * half, 128):
        stats[:, begin : begin + 128] = tile[begin : begin + 128, :].T[:8]


def weigh(at, blocks, logits_own, logits_other):
    tokens, width = blocks[0].shape
    rows = 2 * tokens
    return pl.pallas_call(
        weigh_kernel,
        in_specs=[smem_spec()] + [whole_spec()] * 6,
        out_specs=[whole_spec()] * 3,
        out_shape=[
            jax.ShapeDtypeStruct((rows, width), BF16),
            jax.ShapeDtypeStruct((rows, width), BF16),
            jax.ShapeDtypeStruct((8, 2 * rows), F32),
        ],
        scratch_shapes=[pltpu.VMEM((2 * rows, 128), F32)],
        compiler_params=params(),
        cost_estimate=pl.CostEstimate(
            flops=8 * rows * width, bytes_accessed=16 * rows * width, transcendentals=0
        ),
    )(at, *blocks, logits_own, logits_other)


def matmul_cost(rows, width, features, extra):
    return pl.CostEstimate(
        flops=2 * rows * width * features,
        bytes_accessed=2 * width * (rows + features) + extra,
        transcendentals=0,
    )


def plain_kernel(cotangent, head, out):
    out[...] = lax.dot_general(cotangent[...], head[...], NT, preferred_element_type=F32)


def tile_of(features):
    return 256 if features % 256 == 0 else features


def back_plain(cotangent, head):
    rows, width = cotangent.shape
    features = head.shape[0]
    tile = tile_of(features)
    return pl.pallas_call(
        plain_kernel,
        grid=(features // tile,),
        in_specs=[
            pl.BlockSpec((rows, width), lambda i: (0, 0)),
            pl.BlockSpec((tile, width), lambda i: (i, 0)),
        ],
        out_specs=pl.BlockSpec((rows, tile), lambda i: (0, i)),
        out_shape=jax.ShapeDtypeStruct((rows, features), F32),
        compiler_params=params(),
        cost_estimate=matmul_cost(rows, width, features, 4 * rows * features),
    )(cotangent, head)


def aligned(value, bit):
    if bit % 2 == 0:
        return value
    half = value.shape[1] // 2
    return jnp.concatenate([value[:, half:], value[:, :half]], axis=1)


def columns_of(rows8, out):
    for begin in range(0, rows8.shape[1], 128):
        out[begin : begin + 128, :] = turn(rows8[:, begin : begin + 128])


def stack8(rows):
    pad = jnp.zeros((8 - len(rows), rows[0].shape[1]), F32)
    return jnp.concatenate(rows + [pad], axis=0)


def tilted_kernel(count, cotangent, head, plain, *refs):
    stats, (theirs, kept, joint, columns) = refs[:count], refs[count:]

    @pl.when(pl.program_id(0) == 0)
    def _():
        values = [aligned(stats[bit][...], bit) for bit in range(count)]
        own = values[0]
        row_peak = functools.reduce(jnp.maximum, [value[0:1] for value in values])
        factors = [jnp.exp(value[0:1] - row_peak) for value in values]
        total = sum(f * value[1:2] for f, value in zip(factors, values))
        mean = sum(f * value[1:2] * value[2:3] for f, value in zip(factors, values)) / total
        line = sum(f * value[3:4] for f, value in zip(factors, values)) / total
        tilt = (
            sum(
                f * (value[4:5] + (value[2:3] - mean) * value[3:4])
                for f, value in zip(factors, values)
            )
            / total
        )
        scale = factors[0] / total
        found = stack8([scale, scale * (own[2:3] - mean), line, tilt])
        joint[...] = found
        columns_of(found, columns)

    product = lax.dot_general(cotangent[...], head[...], NT, preferred_element_type=F32)
    result = columns[:, 0:1] * product + columns[:, 1:2] * plain[...]
    half = result.shape[0] // 2
    kept[...] = result[:half]
    theirs[...] = result[half:].astype(BF16)


def weights_kernel(count, cotangent, head, plain, joint, *refs):
    stats, (theirs, kept, sums, columns) = refs[:count], refs[count:]

    @pl.when(pl.program_id(0) == 0)
    def _():
        values = [aligned(stats[bit][...], bit) for bit in range(count)]
        total = sum(value[0:1] for value in values)
        line = sum(value[1:2] for value in values)
        found = stack8([joint[0:1, :], 1.0 / total, line / total])
        sums[...] = found
        columns_of(found, columns)

    product = lax.dot_general(cotangent[...], head[...], NT, preferred_element_type=F32)
    result = columns[:, 0:1] * plain[...] - columns[:, 1:2] * product
    half = result.shape[0] // 2
    kept[...] = result[:half]
    theirs[...] = result[half:].astype(BF16)


def back_scaled(kernel, cotangent, head, plain, first, stats):
    rows, width = cotangent.shape
    features = head.shape[0]
    tile = tile_of(features)
    small = pl.BlockSpec((8, rows), lambda i: (0, 0))
    return pl.pallas_call(
        functools.partial(kernel, len(stats)),
        grid=(features // tile,),
        in_specs=[
            pl.BlockSpec((rows, width), lambda i: (0, 0)),
            pl.BlockSpec((tile, width), lambda i: (i, 0)),
            pl.BlockSpec((rows, tile), lambda i: (0, i)),
        ]
        + [small] * (len(first) + len(stats)),
        out_specs=[
            pl.BlockSpec((rows // 2, tile), lambda i: (0, i)),
            pl.BlockSpec((rows // 2, tile), lambda i: (0, i)),
            small,
        ],
        out_shape=[
            jax.ShapeDtypeStruct((rows // 2, features), BF16),
            jax.ShapeDtypeStruct((rows // 2, features), F32),
            jax.ShapeDtypeStruct((8, rows), F32),
        ],
        scratch_shapes=[pltpu.VMEM((rows, 128), F32)],
        compiler_params=params(),
        cost_estimate=matmul_cost(rows, width, features, 7 * rows * features),
    )(cotangent, head, plain, *first, *stats)


def chain_scatter(part, place, length):
    def right(step):
        return [
            (z * PAIR + y, (z + 1) * PAIR + y)
            for z in range(length - 1)
            for y in range(PAIR)
            if z < step
        ]

    def left(step):
        return [
            ((length - 1 - z) * PAIR + y, (length - 2 - z) * PAIR + y)
            for z in range(length - 1)
            for y in range(PAIR)
            if z < step
        ]

    going_up = going_down = None
    for step in range(1, length):
        up = part(jnp.minimum(length - step + place, length - 1))
        down = part(jnp.maximum(step - length + place, 0))
        if step > 1:
            up = up + going_up.astype(F32)
            down = down + going_down.astype(F32)
        going_up = lax.ppermute(up.astype(BF16), "vocab", right(step))
        going_down = lax.ppermute(down.astype(BF16), "vocab", left(step))
    return part(place) + going_up.astype(F32) + going_down.astype(F32)


def body(hidden, steer, tangent, gain, head, target):
    seq_size = lax.axis_size("seq")
    vocab_size = lax.axis_size("vocab")
    seq_index = lax.axis_index("seq")
    vocab_index = lax.axis_index("vocab")
    tokens, feature_count = hidden.shape
    width = head.shape[0]
    rows = seq_size * tokens
    share = rows // vocab_size
    quarter = tokens // QUARTERS
    size = min(share, quarter)
    y, z = vocab_index % PAIR, vocab_index // PAIR
    length = vocab_size // PAIR
    chip = seq_index // 2
    group = 2 * y + z % 2

    def destination(block, begin):
        row = (block % 2) * tokens + begin
        owner, inside = row // share, row % share
        return ((owner % PAIR) ^ y) * tokens + owner // PAIR * share + inside

    starts = jnp.arange(tokens // size) * size
    turned = ((starts // quarter) ^ group) * quarter + starts % quarter

    def places(bits, begins):
        return jnp.concatenate(
            [destination(seq_index ^ bit, begins) for bit in bits]
        ).astype(jnp.int32)

    own_places, other_places = places((0, 1), turned), places((2, 3), turned)
    target_places = places((0, 1, 2, 3), starts)

    at = jnp.stack([seq_index, group]).astype(jnp.int32)
    vectors = jnp.stack([steer, tangent, gain])
    own, mate, near_2, near_3, far_2, far_3, sums_0, parts, two = cut(
        at, hidden, vectors, width, seq_size
    )
    near = jnp.stack([swap(near_2, "seq", 2, seq_size), swap(near_3, "seq", 3, seq_size)])
    mate = swap(mate, "seq", 1, seq_size)
    sums = [sums_0] + [swap(sums_0, "seq", bit, seq_size) for bit in range(1, seq_size)]
    by_y = swap(near, "vocab", 2, vocab_size)
    by_z = swap(near, "vocab", 1, vocab_size)
    far = [swap(far_2, "seq", 2, seq_size), swap(far_3, "seq", 3, seq_size)]
    blocks = [own, mate] + [
        jnp.concatenate([near[i], by_y[i], by_z[i], far[i]], axis=0) for i in range(2)
    ]
    steer_part, gain_part = parts[0], parts[2]

    row = jnp.sum(jnp.dot(two, head, preferred_element_type=F32), axis=0, keepdims=True)
    tangent_row = row
    for bit in range(1, seq_size):
        tangent_row = tangent_row + swap(row, "seq", bit, seq_size)

    denominators = [s[0] / feature_count + EPSILON for s in sums]
    radii = [jnp.sqrt(d) for d in denominators]

    def partial_logits(bit):
        values = blocks[bit].astype(F32) + steer_part
        normed = (gain_part * values / radii[bit][:, None]).astype(BF16)
        return jnp.dot(normed, head, preferred_element_type=F32)

    summed, got = {}, {}
    for base in (0, 2):
        given = swap(partial_logits(base + 1), "seq", 1, seq_size)
        summed[base] = partial_logits(base) + given
        got[base ^ 2] = swap(summed[base].astype(jnp.float16), "seq", 2, seq_size)

    halves = {}
    for base, where in ((2, other_places), (0, own_places)):
        full = summed[base] + got[base].astype(F32)
        mates = swap(full, "seq", 1, seq_size)
        exponent, tilted, logits, stats = soften(
            where, full, mates, tangent_row, sums[base], sums[base + 1], feature_count
        )
        all_stats = [stats] + [
            swap(stats, "vocab", bit, vocab_size) for bit in range(1, vocab_size)
        ]
        plain = back_plain(exponent, head)
        theirs, kept, joint = back_scaled(tilted_kernel, tilted, head, plain, [], all_stats)
        halves[base] = (logits, plain, theirs, kept, joint)

    target_1 = swap(target, "seq", 1, seq_size)
    target_2 = swap(target, "seq", 2, seq_size)
    target_3 = swap(target_2, "seq", 1, seq_size)
    weights_own, weights_other, target_stats = weigh(
        target_places, [target, target_1, target_2, target_3], halves[0][0], halves[2][0]
    )
    target_all = [target_stats] + [
        swap(target_stats, "vocab", bit, vocab_size) for bit in range(1, vocab_size)
    ]
    weighed = {}
    half = rows // 2
    for base, weights in ((2, weights_other), (0, weights_own)):
        begin = 0 if base == 0 else half
        stats = [value[:, begin : begin + half] for value in target_all]
        _, plain, _, _, joint = halves[base]
        weighed[base] = back_scaled(weights_kernel, weights, head, plain, [joint], stats)

    def over_vocab(pairs):
        met = []
        for theirs, kept in pairs:
            met.append(kept + swap(theirs, "vocab", 1, vocab_size).astype(F32))
        joined = jnp.stack(met).reshape(length, share, -1)

        def part(index):
            other = (index // (length // 2)) ^ chip
            place = other * (length // 2) + index % (length // 2)
            return lax.dynamic_index_in_dim(joined, place, 0, False)

        return chain_scatter(part, z, length)

    ggn_mine = over_vocab([halves[base][2:4] for base in (0, 2)])
    grad_mine = over_vocab([weighed[base][0:2] for base in (0, 2)])

    first_row = vocab_index * share
    owner = first_row // tokens
    block = owner ^ seq_index

    def choose(options):
        result = options[0]
        for index in range(1, len(options)):
            result = jnp.where(block == index, options[index], result)
        return result

    def gather_rows(options):
        pieces = []
        for begin in range(0, share, size):
            inside = first_row % tokens + begin
            place = ((inside // quarter) ^ group) * quarter + inside % quarter
            pieces.append(
                choose([lax.dynamic_slice_in_dim(o, place, size, 0) for o in options])
            )
        return jnp.concatenate(pieces, axis=0)

    my_inputs = gather_rows(blocks).astype(F32) + steer_part
    my_denominator = gather_rows(denominators)
    my_radius = jnp.sqrt(my_denominator)
    in_half = z % (length // 2) * share
    other = (z // (length // 2)) ^ chip

    def mine(own_value, other_value):
        value = jnp.where(other == 0, own_value, other_value)
        return lax.dynamic_slice_in_dim(value, in_half, share)

    dot_ggn = mine(halves[0][4][3], halves[2][4][3])
    dot_grad = mine(
        halves[0][4][2] - weighed[0][2][2], halves[2][4][2] - weighed[2][2][2]
    )

    def norm_back(upstream, dotted):
        along = dotted * my_radius / feature_count / my_denominator
        return (gain_part * upstream - my_inputs * along[:, None]) / my_radius[:, None]

    return norm_back(grad_mine, dot_grad), norm_back(ggn_mine, dot_ggn)


def solution(mesh):
    return jax.shard_map(
        body,
        mesh=mesh,
        in_specs=(P("seq", None), P(), P(), P(), P("seq", "vocab"), P("seq", "vocab")),
        out_specs=(P("vocab", "seq"), P("vocab", "seq")),
        check_vma=False,
    )
```

time: 426 us -> 249 us (0.58)
  waiting for transfers between devices: 292 us -> 74.6 us
  starting transfers between devices: 4.47 us -> 78.9 us
  Pallas kernels: 0 us -> 64 us
  blocking collectives: 51.1 us -> 0 us
  other arithmetic: 21.8 us -> 4.7 us
  matrix products: 35.5 us -> 21.9 us
  between operations: 13.9 us -> 1.64 us
  local copies, waits for them, and re-layouts: 6.39 us -> 1.82 us
    reduce_scatter x2 -> x0, waiting for transfers between devices: 232 us -> none  [the longest x1 149 us: body(): lax.psum_scatter(jnp.concatenate([first_part, second_part], axis=1), 'voc...]
    ppermute x0 -> x59, starting transfers between devices: none -> 78.9 us  [the longest x47 52.7 us: swap(): return lax.ppermute(value, axis, [(i, i ^ bit) for i in range(size)])]
    ppermute x0 -> x59, waiting for transfers between devices: none -> 74.6 us  [the longest x47 55.5 us: swap(): return lax.ppermute(value, axis, [(i, i ^ bit) for i in range(size)])]
    pallas_call x0 -> x10, Pallas kernels: none -> 64 us  [the longest x4 34.2 us: back_scaled(): pl.pallas_call(functools.partial(kernel, len(stats)), grid=(features // t...]
    all_gather x1 -> x0, waiting for transfers between devices: 36.6 us -> none  [body(): gathered = lax.all_gather(cotangent, 'seq', axis=0, tiled=True)]
    psum x3 -> x0, blocking collectives: 29.7 us -> none  [the longest x1 17.1 us: body(): lax.psum((jnp.sum(exponent, axis=1), jnp.sum(exponent * dlogits, axis=1),...]
    all_to_all x1 -> x0, waiting for transfers between devices: 23.6 us -> none  [body(): lax.all_to_all(hidden, 'seq', split_axis=1, concat_axis=0, tiled=True)]
    pmax x1 -> x0, blocking collectives: 21.4 us -> none  [body(): row_peak = lax.pmax(local_peak, 'vocab')]
  transfers between devices with their start and end apart: 4 -> 59, of which waited for: 4 -> 19; matrix products, arithmetic and copies ran while one was open for 1% -> 10% of each run, Pallas kernels for 0% -> 25%
where the time goes in v2:
time: 249 us; the launch traced here: 248 us
  starting transfers between devices  78.9 us (32%)
  waiting for transfers between devices  74.6 us (30%)
  Pallas kernels  64 us (26%)
  matrix products  21.9 us (9%)
  other arithmetic  4.7 us (2%)
    ppermute x47, waiting for transfers between devices, swap(): return lax.ppermute(value, axis, [(i, i ^ bit) for i in range(size)])  55.5 us
    ppermute x47, starting transfers between devices, swap(): return lax.ppermute(value, axis, [(i, i ^ bit) for i in range(size)])  52.7 us
    pallas_call x4, Pallas kernels, back_scaled(): pl.pallas_call(functools.partial(kernel, len(stats)), grid=(features // t...  34.2 us
    ppermute x6, starting transfers between devices, chain_scatter(): going_up = lax.ppermute(up.astype(BF16), 'vocab', right(step))  21 us
    dot_general x4, matrix products, partial_logits(): return jnp.dot(normed, head, preferred_element_type=F32)  16.7 us
    pallas_call x2, Pallas kernels, back_plain(): pl.pallas_call(plain_kernel, grid=(features // tile,), in_specs=[pl.Block...  16.5 us
    ppermute x6, waiting for transfers between devices, chain_scatter(): going_down = lax.ppermute(down.astype(BF16), 'vocab', left(step))  13.1 us
    pallas_call x2, Pallas kernels, soften(): pl.pallas_call(functools.partial(soften_kernel, feature_count), in_specs=...  8.16 us
  transfers between devices with their start and end apart: 59, of which 19 were waited for; matrix products, arithmetic and copies ran while one was open for 10% of the time, Pallas kernels for 25%

profile of v2, /device:TPU:0, one launch (start us, length us, event | category | flops | bytes accessed | tf_op | source)
XLA Modules:
  0.0 247.6 jit_solution(3167842940036418592)
XLA Ops:
  7.9 5.2 %convolution_reduce_fusion = f32[2432]{0:T(1024)S(1)} fusion(bf16[16,2048]{1,0:T(8,128)(2,1)S(1)} %get-tuple-element.42, bf16[2048,2432]{1,0:T(8,128)(2,1)} %head.11), kind=kOutput, calls=%fused_computation.6 | convolution fusion | flops 159420032 | bytes 10036736 | tf_op jit(solution)/shard_map/dot_general | solution.py:426
  25.1 5.6 %fusion = f32[128,2432]{1,0:T(8,128)S(1)} fusion(bf16[2048,2432]{1,0:T(8,128)(2,1)} %head.11, bf16[128,2048]{1,0:T(8,128)(2,1)S(1)} %collective-permute-done.3, f32[128]{0:T(128)S(1)} %get-tuple-element.111, f32[2048]{0:T(1024)S(1)} %bitcast.140, f32[2048]{0:T(1024)S(1)} %bitcast.135), kind=kOutput, calls=%fused_computation.15 | convolution fusion | flops 1276379136 | bytes 11747840 | tf_op jit(solution)/shard_map/dot_general | solution.py:437
  32.4 5.8 %collective-permute-done.12 = bf16[32,2048]{1,0:T(8,128)(2,1)S(1)} collective-permute-done((bf16[32,2048]{1,0:T(8,128)(2,1)S(1)}, bf16[32,2048]{1,0:T(8,128)(2,1)S(1)}, u32[]{:S(2)}, u32[]{:S(2)}) %collective-permute-start.12) | collective-permute-done | bytes 131104 | tf_op jit(solution)/shard_map/ppermute | solution.py:31
  45.9 16.9 %collective-permute-done.10 = bf16[32,2048]{1,0:T(8,128)(2,1)S(1)} collective-permute-done((bf16[32,2048]{1,0:T(8,128)(2,1)S(1)}, bf16[32,2048]{1,0:T(8,128)(2,1)S(1)}, u32[]{:S(2)}, u32[]{:S(2)}) %collective-permute-start.10) | collective-permute-done | bytes 131104 | tf_op jit(solution)/shard_map/ppermute | solution.py:31
  62.8 6.0 %convert_add_fusion = (f32[128,2432]{1,0:T(8,128)S(1)}, f16[128,2432]{1,0:T(8,128)(2,1)S(1)}) fusion(f16[128,2432]{1,0:T(8,128)(2,1)} %collective-permute-done.20, f32[128,2432]{1,0:T(8,128)} %collective-permute-done.14, bf16[2048,2432]{1,0:T(8,128)(2,1)} %head.11, f32[128]{0:T(128)S(1)} %get-tuple-element.109, f32[2048]{0:T(1024)S(1)} %bitcast.143, ...), kind=kOutput, calls=%fused_computation.4 | convolution fusion | flops 1279459328 | bytes 14238208 | tf_op jit(solution)/shard_map/dot_general | solution.py:437
  71.9 4.1 %shard_map.79 = (bf16[256,2432]{1,0:T(8,128)(2,1)S(1)}, bf16[256,2432]{1,0:T(8,128)(2,1)S(1)}, f32[256,2432]{1,0:T(8,128)}, f32[8,256]{1,0:T(8,128)S(1)}) custom-call(s32[8]{0:T(128)S(1)} %pad_add_fusion.3.at, f32[128,2432]{1,0:T(8,128)S(1)} %get-tuple-element.76.first, f32[128,2432]{1,0:T(8,128)S(1)} %collective-permute-done.21.second, ...), custom_call_target="tpu_custom_call" | custom-call | flops 18677760 | bytes 7471104 | tf_op jit(solution)/shard_map/pallas_call | solution.py:148
  79.7 5.8 %collective-permute-done.15 = f16[128,2432]{1,0:T(8,128)(2,1)S(1)} collective-permute-done((f16[128,2432]{1,0:T(8,128)(2,1)S(1)}, f16[128,2432]{1,0:T(8,128)(2,1)S(1)}, u32[]{:S(2)}, u32[]{:S(2)}) %collective-permute-start.15) | collective-permute-done | bytes 622624 | tf_op jit(solution)/shard_map/ppermute | solution.py:31
  92.0 8.3 %shard_map.84.plain = f32[256,2048]{1,0:T(8,128)S(1)} custom-call(bf16[256,2432]{1,0:T(8,128)(2,1)S(1)} %get-tuple-element.54.cotangent, bf16[2048,2432]{1,0:T(8,128)(2,1)} %head.11), custom_call_target="tpu_custom_call" | custom-call | flops 2550136832 | bytes 13303808 | tf_op jit(solution)/shard_map/pallas_call | solution.py:238
  101.2 8.6 %shard_map.85 = (bf16[128,2048]{1,0:T(8,128)(2,1)S(1)}, f32[128,2048]{1,0:T(8,128)S(1)}, f32[8,256]{1,0:T(8,128)S(1)}) custom-call(bf16[256,2432]{1,0:T(8,128)(2,1)S(1)} %get-tuple-element.55.cotangent, bf16[2048,2432]{1,0:T(8,128)(2,1)} %head.11, f32[256,2048]{1,0:T(8,128)S(1)} %shard_map.84.plain, f32[8,256]{1,0:T(8,128)S(1)} %get-tuple-element.56.refs_0_, ...), custom_call_target="tpu_custom_call" | custom-call | flops 2550136832 | bytes 14876672 | tf_op jit(solution)/shard_map/pallas_call | solution.py:324
  111.9 4.9 %collective-permute-done.1.refs_2_ = bf16[128,2432]{1,0:T(8,128)(2,1)S(1)} collective-permute-done((bf16[128,2432]{1,0:T(8,128)(2,1)S(1)}, bf16[128,2432]{1,0:T(8,128)(2,1)S(1)}, u32[]{:S(2)}, u32[]{:S(2)}) %collective-permute-start.1) | collective-permute-done | bytes 622624 | tf_op jit(solution)/shard_map/ppermute | solution.py:31
  116.8 7.2 %collective-permute-done.52 = bf16[128,2048]{1,0:T(8,128)(2,1)S(1)} collective-permute-done((bf16[128,2048]{1,0:T(8,128)(2,1)S(1)}, bf16[128,2048]{1,0:T(8,128)(2,1)S(1)}, u32[]{:S(2)}, u32[]{:S(2)}) %collective-permute-start.52) | collective-permute-done | bytes 524320 | tf_op jit(solution)/shard_map/ppermute | solution.py:31
  128.1 4.8 %collective-permute-start.28 = (f32[8,256]{1,0:T(8,128)S(1)}, f32[8,256]{1,0:T(8,128)S(1)}, u32[]{:S(2)}, u32[]{:S(2)}) collective-permute-start(f32[8,256]{1,0:T(8,128)S(1)} %get-tuple-element.48.refs_0_), channel_id=1, source_target_pairs={{0,7},{1,6},{2,5},{3,4},{4,3},{5,2},{6,1},{7,0},{8,15},{9,14},{10,... | collective-permute-start | bytes 24584 | tf_op jit(solution)/shard_map/ppermute | solution.py:31
  133.6 8.2 %shard_map.81.plain = f32[256,2048]{1,0:T(8,128)S(1)} custom-call(bf16[256,2432]{1,0:T(8,128)(2,1)S(1)} %get-tuple-element.46.cotangent, bf16[2048,2432]{1,0:T(8,128)(2,1)} %head.11), custom_call_target="tpu_custom_call" | custom-call | flops 2550136832 | bytes 13303808 | tf_op jit(solution)/shard_map/pallas_call | solution.py:238
  151.4 4.7 %collective-permute-start.35 = (f32[8,512]{1,0:T(8,128)S(1)}, f32[8,512]{1,0:T(8,128)S(1)}, u32[]{:S(2)}, u32[]{:S(2)}) collective-permute-start(f32[8,512]{1,0:T(8,128)S(1)} %get-tuple-element.50), channel_id=1, source_target_pairs={{0,7},{1,6},{2,5},{3,4},{4,3},{5,2},{6,1},{7,0},{8,15},{9,14},{10,... | collective-permute-start | bytes 49160 | tf_op jit(solution)/shard_map/ppermute | solution.py:31
  161.4 8.6 %shard_map.82 = (bf16[128,2048]{1,0:T(8,128)(2,1)S(1)}, f32[128,2048]{1,0:T(8,128)S(1)}, f32[8,256]{1,0:T(8,128)S(1)}) custom-call(bf16[256,2432]{1,0:T(8,128)(2,1)S(1)} %get-tuple-element.47.cotangent, bf16[2048,2432]{1,0:T(8,128)(2,1)} %head.11, f32[256,2048]{1,0:T(8,128)S(1)} %shard_map.81.plain, f32[8,256]{1,0:T(8,128)S(1)} %get-tuple-element.48.refs_0_, ...), custom_call_target="tpu_custom_call" | custom-call | flops 2550136832 | bytes 14876672 | tf_op jit(solution)/shard_map/pallas_call | solution.py:324
  174.8 8.5 %shard_map.86 = (bf16[128,2048]{1,0:T(8,128)(2,1)S(1)}, f32[128,2048]{1,0:T(8,128)S(1)}, f32[8,256]{1,0:T(8,128)S(1)}) custom-call(bf16[256,2432]{1,0:T(8,128)(2,1)S(1)} %get-tuple-element.53.cotangent, bf16[2048,2432]{1,0:T(8,128)(2,1)} %head.11, f32[256,2048]{1,0:T(8,128)S(1)} %shard_map.84.plain, f32[8,256]{1,0:T(8,128)S(1)} %get-tuple-element.57.joint, ...), custom_call_target="tpu_custom_call" | custom-call | flops 2550136832 | bytes 14876672 | tf_op jit(solution)/shard_map/pallas_call | solution.py:324
  183.8 8.5 %shard_map.83 = (bf16[128,2048]{1,0:T(8,128)(2,1)S(1)}, f32[128,2048]{1,0:T(8,128)S(1)}, f32[8,256]{1,0:T(8,128)S(1)}) custom-call(bf16[256,2432]{1,0:T(8,128)(2,1)S(1)} %get-tuple-element.45.cotangent, bf16[2048,2432]{1,0:T(8,128)(2,1)} %head.11, f32[256,2048]{1,0:T(8,128)S(1)} %shard_map.81.plain, f32[8,256]{1,0:T(8,128)S(1)} %get-tuple-element.49.joint, ...), custom_call_target="tpu_custom_call" | custom-call | flops 2550136832 | bytes 14876672 | tf_op jit(solution)/shard_map/pallas_call | solution.py:324
  198.5 5.3 %collective-permute-done.36 = bf16[128,2048]{1,0:T(8,128)(2,1)S(1)} collective-permute-done((bf16[128,2048]{1,0:T(8,128)(2,1)S(1)}, bf16[128,2048]{1,0:T(8,128)(2,1)S(1)}, u32[]{:S(2)}, u32[]{:S(2)}) %collective-permute-start.36) | collective-permute-done | bytes 524320 | tf_op jit(solution)/shard_map/ppermute | solution.py:31
  209.5 4.1 %collective-permute-done.45 = bf16[64,2048]{1,0:T(8,128)(2,1)S(1)} collective-permute-done((bf16[64,2048]{1,0:T(8,128)(2,1)S(1)}, bf16[64,2048]{1,0:T(8,128)(2,1)S(1)}, u32[]{:S(2)}, u32[]{:S(2)}) %collective-permute-start.45) | collective-permute-done | bytes 262176 | tf_op jit(solution)/shard_map/ppermute | solution.py:373
  213.6 4.4 %collective-permute-start.46 = (bf16[64,2048]{1,0:T(8,128)(2,1)S(1)}, bf16[64,2048]{1,0:T(8,128)(2,1)S(1)}, u32[]{:S(2)}, u32[]{:S(2)}) collective-permute-start(bf16[64,2048]{1,0:T(8,128)(2,1)S(1)} %fusion.12), channel_id=1, source_target_pairs={{0,2},{1,3},{2,4},{3,5},{8,10},{9,11},{10,12},{11,13},{16,18},{17,... | collective-permute-start | bytes 786440 | tf_op jit(solution)/shard_map/ppermute | solution.py:373
  219.3 4.4 %collective-permute-start.55 = (bf16[64,2048]{1,0:T(8,128)(2,1)S(1)}, bf16[64,2048]{1,0:T(8,128)(2,1)S(1)}, u32[]{:S(2)}, u32[]{:S(2)}) collective-permute-start(bf16[64,2048]{1,0:T(8,128)(2,1)S(1)} %get-tuple-element.66), channel_id=1, source_target_pairs={{0,2},{1,3},{2,4},{3,5},{4,6},{5,7},{8,10},{9,11},{10,12},{11,13},... | collective-permute-start | bytes 786440 | tf_op jit(solution)/shard_map/ppermute | solution.py:373
  224.9 4.4 %collective-permute-start.47 = (bf16[64,2048]{1,0:T(8,128)(2,1)S(1)}, bf16[64,2048]{1,0:T(8,128)(2,1)S(1)}, u32[]{:S(2)}, u32[]{:S(2)}) collective-permute-start(bf16[64,2048]{1,0:T(8,128)(2,1)S(1)} %get-tuple-element.72), channel_id=1, source_target_pairs={{0,2},{1,3},{2,4},{3,5},{4,6},{5,7},{8,10},{9,11},{10,12},{11,13},... | collective-permute-start | bytes 786440 | tf_op jit(solution)/shard_map/ppermute | solution.py:373
  233.2 8.0 %collective-permute-done.58 = bf16[64,2048]{1,0:T(8,128)(2,1)S(1)} collective-permute-done((bf16[64,2048]{1,0:T(8,128)(2,1)S(1)}, bf16[64,2048]{1,0:T(8,128)(2,1)S(1)}, u32[]{:S(2)}, u32[]{:S(2)}) %collective-permute-start.58) | collective-permute-done | bytes 262176 | tf_op jit(solution)/shard_map/ppermute | solution.py:374
  241.2 5.1 %collective-permute-done.50 = bf16[64,2048]{1,0:T(8,128)(2,1)S(1)} collective-permute-done((bf16[64,2048]{1,0:T(8,128)(2,1)S(1)}, bf16[64,2048]{1,0:T(8,128)(2,1)S(1)}, u32[]{:S(2)}, u32[]{:S(2)}) %collective-permute-start.50) | collective-permute-done | bytes 262176 | tf_op jit(solution)/shard_map/ppermute | solution.py:374
  (172 shorter events, 88.5 us)
Async XLA Ops:
  7.2 37.0 %collective-permute-start.11 = (f32[8,128]{1,0:T(8,128)S(1)}, f32[8,128]{1,0:T(8,128)S(1)}, u32[]{:S(2)}, u32[]{:S(2)}) collective-permute-start(f32[8,128]{1,0:T(8,128)S(1)} %get-tuple-element.36.sums_a), channel_id=1, source_target_pairs={{0,16},{8,24},{16,0},{24,8},{1,17},{9,25},{17,1},{25,9},{2,18},{10... | collective-permute-start | bytes 12296 | tf_op jit(solution)/shard_map/ppermute | solution.py:31
  13.2 57.0 %collective-permute-start.18 = (f32[1,2432]{1,0:T(1,128)S(1)}, f32[1,2432]{1,0:T(1,128)S(1)}, u32[]{:S(2)}, u32[]{:S(2)}) collective-permute-start(f32[1,2432]{1,0:T(1,128)S(1)} %broadcast_in_dim.2), channel_id=1, source_target_pairs={{0,16},{8,24},{16,0},{24,8},{1,17},{9,25},{17,1},{25,9},{2,18},{10... | collective-permute-start | bytes 29192 | tf_op jit(solution)/shard_map/ppermute | solution.py:31
  21.4 48.8 %collective-permute-start.19 = (f32[1,2432]{1,0:T(1,128)S(1)}, f32[1,2432]{1,0:T(1,128)S(1)}, u32[]{:S(2)}, u32[]{:S(2)}) collective-permute-start(f32[1,2432]{1,0:T(1,128)S(1)} %broadcast_in_dim.2), channel_id=1, source_target_pairs={{0,24},{8,16},{16,8},{24,0},{1,25},{9,17},{17,9},{25,1},{2,26},{10... | collective-permute-start | bytes 29192 | tf_op jit(solution)/shard_map/ppermute | solution.py:31
  40.8 22.0 %collective-permute-start.14 = (f32[128,2432]{1,0:T(8,128)}, f32[128,2432]{1,0:T(8,128)}, u32[]{:S(2)}, u32[]{:S(2)}) collective-permute-start(f32[128,2432]{1,0:T(8,128)} %fusion.1), channel_id=1, source_target_pairs={{0,8},{8,0},{16,24},{24,16},{1,9},{9,1},{17,25},{25,17},{2,10},{10... | collective-permute-start | bytes 3735560 | tf_op jit(solution)/shard_map/ppermute | solution.py:31
  43.4 19.4 %collective-permute-start.20 = (f16[128,2432]{1,0:T(8,128)(2,1)}, f16[128,2432]{1,0:T(8,128)(2,1)}, u32[]{:S(2)}, u32[]{:S(2)}) collective-permute-start(f16[128,2432]{1,0:T(8,128)(2,1)} %get-tuple-element.119), channel_id=1, source_target_pairs={{0,16},{8,24},{16,0},{24,8},{1,17},{9,25},{17,1},{25,9},{2,18},{10... | collective-permute-start | bytes 1867784 | tf_op jit(solution)/shard_map/ppermute | solution.py:31
  44.3 18.5 %collective-permute-start.10 = (bf16[32,2048]{1,0:T(8,128)(2,1)S(1)}, bf16[32,2048]{1,0:T(8,128)(2,1)S(1)}, u32[]{:S(2)}, u32[]{:S(2)}) collective-permute-start(bf16[32,2048]{1,0:T(8,128)(2,1)S(1)} %get-tuple-element.40), channel_id=1, source_target_pairs={{0,16},{8,24},{16,0},{24,8},{1,17},{9,25},{17,1},{25,9},{2,18},{10... | collective-permute-start | bytes 393224 | tf_op jit(solution)/shard_map/ppermute | solution.py:31
  69.6 16.0 %collective-permute-start.15 = (f16[128,2432]{1,0:T(8,128)(2,1)S(1)}, f16[128,2432]{1,0:T(8,128)(2,1)S(1)}, u32[]{:S(2)}, u32[]{:S(2)}) collective-permute-start(f16[128,2432]{1,0:T(8,128)(2,1)S(1)} %get-tuple-element.77), channel_id=1, source_target_pairs={{0,16},{8,24},{16,0},{24,8},{1,17},{9,25},{17,1},{25,9},{2,18},{10... | collective-permute-start | bytes 1867784 | tf_op jit(solution)/shard_map/ppermute | solution.py:31
  76.1 15.1 %collective-permute-start.43 = (f32[8,256]{1,0:T(8,128)S(1)}, f32[8,256]{1,0:T(8,128)S(1)}, u32[]{:S(2)}, u32[]{:S(2)}) collective-permute-start(f32[8,256]{1,0:T(8,128)S(1)} %get-tuple-element.56.refs_0_), channel_id=1, source_target_pairs={{0,7},{1,6},{2,5},{3,4},{4,3},{5,2},{6,1},{7,0},{8,15},{9,14},{10,... | collective-permute-start | bytes 24584 | tf_op jit(solution)/shard_map/ppermute | solution.py:31
  100.3 41.6 %collective-permute-start = (bf16[128,2432]{1,0:T(8,128)(2,1)S(1)}, bf16[128,2432]{1,0:T(8,128)(2,1)S(1)}, u32[]{:S(2)}, u32[]{:S(2)}) collective-permute-start(bf16[128,2432]{1,0:T(8,128)(2,1)S(1)} %copy-done.1), channel_id=1, source_target_pairs={{0,8},{8,0},{16,24},{24,16},{1,9},{9,1},{17,25},{25,17},{2,10},{10... | collective-permute-start | bytes 1867784 | tf_op jit(solution)/shard_map/ppermute | solution.py:31
  100.4 16.4 %collective-permute-start.1 = (bf16[128,2432]{1,0:T(8,128)(2,1)S(1)}, bf16[128,2432]{1,0:T(8,128)(2,1)S(1)}, u32[]{:S(2)}, u32[]{:S(2)}) collective-permute-start(bf16[128,2432]{1,0:T(8,128)(2,1)S(1)} %copy-done.1), channel_id=1, source_target_pairs={{0,16},{8,24},{16,0},{24,8},{1,17},{9,25},{17,1},{25,9},{2,18},{10... | collective-permute-start | bytes 1867784 | tf_op jit(solution)/shard_map/ppermute | solution.py:31
  101.0 23.1 %collective-permute-start.16 = (f32[128,2432]{1,0:T(8,128)S(1)}, f32[128,2432]{1,0:T(8,128)S(1)}, u32[]{:S(2)}, u32[]{:S(2)}) collective-permute-start(f32[128,2432]{1,0:T(8,128)S(1)} %convert_add_fusion.1.first), channel_id=1, source_target_pairs={{0,8},{8,0},{16,24},{24,16},{1,9},{9,1},{17,25},{25,17},{2,10},{10... | collective-permute-start | bytes 3735560 | tf_op jit(solution)/shard_map/ppermute | solution.py:31
  116.8 27.3 %collective-permute-start.2 = (bf16[128,2432]{1,0:T(8,128)(2,1)S(1)}, bf16[128,2432]{1,0:T(8,128)(2,1)S(1)}, u32[]{:S(2)}, u32[]{:S(2)}) collective-permute-start(bf16[128,2432]{1,0:T(8,128)(2,1)S(1)} %collective-permute-done.1.refs_2_), channel_id=1, source_target_pairs={{0,8},{8,0},{16,24},{24,16},{1,9},{9,1},{17,25},{25,17},{2,10},{10... | collective-permute-start | bytes 1867784 | tf_op jit(solution)/shard_map/ppermute | solution.py:31
  128.1 22.1 %collective-permute-start.28 = (f32[8,256]{1,0:T(8,128)S(1)}, f32[8,256]{1,0:T(8,128)S(1)}, u32[]{:S(2)}, u32[]{:S(2)}) collective-permute-start(f32[8,256]{1,0:T(8,128)S(1)} %get-tuple-element.48.refs_0_), channel_id=1, source_target_pairs={{0,7},{1,6},{2,5},{3,4},{4,3},{5,2},{6,1},{7,0},{8,15},{9,14},{10,... | collective-permute-start | bytes 24584 | tf_op jit(solution)/shard_map/ppermute | solution.py:31
  132.9 18.1 %collective-permute-start.27 = (f32[8,256]{1,0:T(8,128)S(1)}, f32[8,256]{1,0:T(8,128)S(1)}, u32[]{:S(2)}, u32[]{:S(2)}) collective-permute-start(f32[8,256]{1,0:T(8,128)S(1)} %get-tuple-element.48.refs_0_), channel_id=1, source_target_pairs={{0,6},{1,7},{2,4},{3,5},{4,2},{5,3},{6,0},{7,1},{8,14},{9,15},{10,... | collective-permute-start | bytes 24584 | tf_op jit(solution)/shard_map/ppermute | solution.py:31
  133.1 18.2 %collective-permute-start.26 = (f32[8,256]{1,0:T(8,128)S(1)}, f32[8,256]{1,0:T(8,128)S(1)}, u32[]{:S(2)}, u32[]{:S(2)}) collective-permute-start(f32[8,256]{1,0:T(8,128)S(1)} %get-tuple-element.48.refs_0_), channel_id=1, source_target_pairs={{0,5},{1,4},{2,7},{3,6},{4,1},{5,0},{6,3},{7,2},{8,13},{9,12},{10,... | collective-permute-start | bytes 24584 | tf_op jit(solution)/shard_map/ppermute | solution.py:31
  151.4 18.7 %collective-permute-start.35 = (f32[8,512]{1,0:T(8,128)S(1)}, f32[8,512]{1,0:T(8,128)S(1)}, u32[]{:S(2)}, u32[]{:S(2)}) collective-permute-start(f32[8,512]{1,0:T(8,128)S(1)} %get-tuple-element.50), channel_id=1, source_target_pairs={{0,7},{1,6},{2,5},{3,4},{4,3},{5,2},{6,1},{7,0},{8,15},{9,14},{10,... | collective-permute-start | bytes 49160 | tf_op jit(solution)/shard_map/ppermute | solution.py:31
  156.1 14.7 %collective-permute-start.34 = (f32[8,512]{1,0:T(8,128)S(1)}, f32[8,512]{1,0:T(8,128)S(1)}, u32[]{:S(2)}, u32[]{:S(2)}) collective-permute-start(f32[8,512]{1,0:T(8,128)S(1)} %get-tuple-element.50), channel_id=1, source_target_pairs={{0,6},{1,7},{2,4},{3,5},{4,2},{5,3},{6,0},{7,1},{8,14},{9,15},{10,... | collective-permute-start | bytes 49160 | tf_op jit(solution)/shard_map/ppermute | solution.py:31
  156.3 14.9 %collective-permute-start.33 = (f32[8,512]{1,0:T(8,128)S(1)}, f32[8,512]{1,0:T(8,128)S(1)}, u32[]{:S(2)}, u32[]{:S(2)}) collective-permute-start(f32[8,512]{1,0:T(8,128)S(1)} %get-tuple-element.50), channel_id=1, source_target_pairs={{0,5},{1,4},{2,7},{3,6},{4,1},{5,0},{6,3},{7,2},{8,13},{9,12},{10,... | collective-permute-start | bytes 49160 | tf_op jit(solution)/shard_map/ppermute | solution.py:31
  156.7 16.2 %collective-permute-start.32 = (f32[8,512]{1,0:T(8,128)S(1)}, f32[8,512]{1,0:T(8,128)S(1)}, u32[]{:S(2)}, u32[]{:S(2)}) collective-permute-start(f32[8,512]{1,0:T(8,128)S(1)} %get-tuple-element.50), channel_id=1, source_target_pairs={{0,4},{1,5},{2,6},{3,7},{4,0},{5,1},{6,2},{7,3},{8,12},{9,13},{10,... | collective-permute-start | bytes 49160 | tf_op jit(solution)/shard_map/ppermute | solution.py:31
  171.2 22.8 %collective-permute-start.51 = (bf16[128,2048]{1,0:T(8,128)(2,1)S(1)}, bf16[128,2048]{1,0:T(8,128)(2,1)S(1)}, u32[]{:S(2)}, u32[]{:S(2)}) collective-permute-start(bf16[128,2048]{1,0:T(8,128)(2,1)S(1)} %get-tuple-element.63), channel_id=1, source_target_pairs={{0,1},{1,0},{2,3},{3,2},{4,5},{5,4},{6,7},{7,6},{8,9},{9,8},{10,11... | collective-permute-start | bytes 1572872 | tf_op jit(solution)/shard_map/ppermute | solution.py:31
  183.3 15.0 %collective-permute-start.44 = (bf16[128,2048]{1,0:T(8,128)(2,1)S(1)}, bf16[128,2048]{1,0:T(8,128)(2,1)S(1)}, u32[]{:S(2)}, u32[]{:S(2)}) collective-permute-start(bf16[128,2048]{1,0:T(8,128)(2,1)S(1)} %get-tuple-element.59), channel_id=1, source_target_pairs={{0,1},{1,0},{2,3},{3,2},{4,5},{5,4},{6,7},{7,6},{8,9},{9,8},{10,11... | collective-permute-start | bytes 1572872 | tf_op jit(solution)/shard_map/ppermute | solution.py:31
  197.7 20.3 %collective-permute-start.56 = (bf16[64,2048]{1,0:T(8,128)(2,1)S(1)}, bf16[64,2048]{1,0:T(8,128)(2,1)S(1)}, u32[]{:S(2)}, u32[]{:S(2)}) collective-permute-start(bf16[64,2048]{1,0:T(8,128)(2,1)S(1)} %get-tuple-element.69), channel_id=1, source_target_pairs={{6,4},{7,5},{14,12},{15,13},{22,20},{23,21},{30,28},{31,29}} | collective-permute-start | bytes 786440 | tf_op jit(solution)/shard_map/ppermute | solution.py:374
  207.4 17.0 %collective-permute-start.48 = (bf16[64,2048]{1,0:T(8,128)(2,1)S(1)}, bf16[64,2048]{1,0:T(8,128)(2,1)S(1)}, u32[]{:S(2)}, u32[]{:S(2)}) collective-permute-start(bf16[64,2048]{1,0:T(8,128)(2,1)S(1)} %get-tuple-element.75), channel_id=1, source_target_pairs={{6,4},{7,5},{14,12},{15,13},{22,20},{23,21},{30,28},{31,29}} | collective-permute-start | bytes 786440 | tf_op jit(solution)/shard_map/ppermute | solution.py:374
  231.5 14.8 %collective-permute-start.50 = (bf16[64,2048]{1,0:T(8,128)(2,1)S(1)}, bf16[64,2048]{1,0:T(8,128)(2,1)S(1)}, u32[]{:S(2)}, u32[]{:S(2)}) collective-permute-start(bf16[64,2048]{1,0:T(8,128)(2,1)S(1)} %fusion.11), channel_id=1, source_target_pairs={{6,4},{7,5},{4,2},{5,3},{2,0},{3,1},{14,12},{15,13},{12,10},{13,11... | collective-permute-start | bytes 786440 | tf_op jit(solution)/shard_map/ppermute | solution.py:374
  (40 other events, 381.8 us)
